TPU v7x, 32 devices: a whole 2x2x4 slice. The times are simulated.
32 devices in a mesh: slab: 8 (over z, y), dom: 4 (over x, core).
Axes of the slice: x: 2, y: 2, z: 4, core: 2. Of those that a mesh axis runs over, the one named last changes fastest.
Arguments:
- atom_features: bfloat16 [4096, 3200], P(('slab', 'dom')), may hold values from -6 to 6
- halo_lists: int32 [8, 32, 8], P(None, ('slab', 'dom')), may hold values from 0 to 127, as said below
- probe_atoms: int32 [8, 8192], P(None, ('slab', 'dom')), may hold values from -1 to 255, as said below
- offsets: float32 [3, 8, 8192], P(None, None, ('slab', 'dom')), may hold values from -4 to 4, as said below
- radial_weights: float32 [8, 640], replicated, may hold values from -4 to 4
- probe_weight: float32 [128, 128], replicated, may hold values from -0.5 to 0.5
- out_weight: float32 [128], replicated, may hold values from -0.5 to 0.5
- density_cotangent: float32 [8192], P(('slab', 'dom')), may hold values from -6 to 6
Outputs:
- density: float32 [8192], P(('slab', 'dom'))
- atom_grads: float32 [4096, 3200], P(('slab', 'dom'))
Inputs may be any that keep to these rules, and one draw needn't show every extreme that they name: `halo_lists`: within one slab and one owner the listed local atom numbers are distinct. `probe_atoms`: -1 marks an empty slot; any other entry is a row of the probe's slab table of 256 rows. Row t belongs to owner t // 8. Among the slots of the probes of one device, at most 64 live ones name rows of one owner; in every draw some owner is named by exactly 64 live slots from every device. `offsets`: every displacement has a length between 0.5 and 4.
All inputs are finite; a program needn't handle non-finite values.
Results may differ from a plain program's by a relative error of at most 0.0041.
Values may be sent and summed in bfloat16 or wider, within the bound.
No kernel may reach another device: no remote copies, remote signals or barrier semaphores. Data moves between devices by JAX's collectives and lax.ppermute only.
A program may use at most 128 MiB of HBM per device.

v0:
```python
import jax
import jax.numpy as jnp
from jax import lax
from jax.sharding import PartitionSpec as P

cutoff_radius = 4.0
item_block = 512


def harmonics(xcoord, ycoord, zcoord):
    xsq = xcoord * xcoord
    ysq = ycoord * ycoord
    zsq = zcoord * zcoord
    values = [
        0.28209479 * jnp.ones_like(xcoord),
        0.48860251 * ycoord,
        0.48860251 * zcoord,
        0.48860251 * xcoord,
        1.09254843 * xcoord * ycoord,
        1.09254843 * ycoord * zcoord,
        0.31539157 * (3.0 * zsq - 1.0),
        1.09254843 * xcoord * zcoord,
        0.54627422 * (xsq - ysq),
        0.59004359 * ycoord * (3.0 * xsq - ysq),
        2.89061144 * xcoord * ycoord * zcoord,
        0.4570458 * ycoord * (5.0 * zsq - 1.0),
        0.37317633 * zcoord * (5.0 * zsq - 3.0),
        0.4570458 * xcoord * (5.0 * zsq - 1.0),
        1.44530572 * zcoord * (xsq - ysq),
        0.59004359 * xcoord * (xsq - 3.0 * ysq),
        2.50334294 * xcoord * ycoord * (xsq - ysq),
        1.77013077 * ycoord * zcoord * (3.0 * xsq - ysq),
        0.9461747 * xcoord * ycoord * (7.0 * zsq - 1.0),
        0.66904654 * ycoord * zcoord * (7.0 * zsq - 3.0),
        0.10578555 * (35.0 * zsq * zsq - 30.0 * zsq + 3.0),
        0.66904654 * xcoord * zcoord * (7.0 * zsq - 3.0),
        0.47308735 * (xsq - ysq) * (7.0 * zsq - 1.0),
        1.77013077 * xcoord * zcoord * (xsq - 3.0 * ysq),
        0.62583574 * (xsq * (xsq - 3.0 * ysq) - ysq * (3.0 * xsq - ysq)),
    ]
    return jnp.stack(values, axis=-1)


def geometry(offset_block, radial_weights):
    length = jnp.sqrt(jnp.sum(offset_block * offset_block, axis=0))
    orders = jnp.arange(1, radial_weights.shape[0] + 1).astype(length.dtype)
    envelope = 0.5 * (jnp.cos(jnp.pi * length / cutoff_radius) + 1.0)
    basis = (
        jnp.sqrt(2.0 / cutoff_radius)
        * jnp.sin(orders * jnp.pi * length[..., None] / cutoff_radius)
        / length[..., None]
        * envelope[..., None]
    )
    slots, probes = length.shape
    channels = radial_weights.shape[1] // 5
    radial = jnp.dot(
        basis.reshape(-1, basis.shape[-1]), radial_weights, precision=lax.Precision.HIGHEST
    ).reshape(slots, probes, 5, channels)
    unit = offset_block / length[None]
    harmonic = harmonics(unit[0], unit[1], unit[2]).astype(jnp.bfloat16)
    return (radial, harmonic)


def contract_sums(gathered, harmonic, radial, alive_mask):
    summed = jnp.zeros((gathered.shape[1], gathered.shape[3]), jnp.float32)
    for degree in range(5):
        part_y = harmonic[:, :, degree * degree : (degree + 1) ** 2]
        part_h = gathered[:, :, degree * degree : (degree + 1) ** 2, :]
        contracted = jnp.einsum("kpm,kpmc->kpc", part_y, part_h, preferred_element_type=jnp.float32)
        summed = summed + jnp.sum(radial[:, :, degree] * contracted * alive_mask[..., None], axis=0)
    return summed


def readout(summed, probe_weight, out_weight, cot_block):
    preact = jnp.dot(summed, probe_weight, precision=lax.Precision.HIGHEST)
    density = jnp.dot(jax.nn.silu(preact), out_weight, precision=lax.Precision.HIGHEST)
    sigma = jax.nn.sigmoid(preact)
    dpre = cot_block[:, None] * out_weight[None, :] * sigma * (1.0 + preact * (1.0 - sigma))
    dsum = jnp.dot(dpre, probe_weight.T, precision=lax.Precision.HIGHEST)
    return (density, dsum)


def slot_grads(harmonic, radial, weighted):
    pieces = []
    for degree in range(5):
        part_y = harmonic[:, :, degree * degree : (degree + 1) ** 2].astype(jnp.float32)
        pieces.append(part_y[..., None] * (weighted * radial[:, :, degree])[:, :, None, :])
    return jnp.concatenate(pieces, axis=2)


def shards(
    atom_features,
    halo_lists,
    probe_atoms,
    offsets,
    radial_weights,
    probe_weight,
    out_weight,
    density_cotangent,
):
    n_slab = lax.axis_size("slab")
    n_dom = lax.axis_size("dom")
    devices = n_slab * n_dom
    feature_len = atom_features.shape[1]
    channels = feature_len // 25
    slots_per = probe_atoms.shape[0]
    probe_count = probe_atoms.shape[1]
    total = slots_per * probe_count
    hslot = halo_lists.shape[2]
    slot_cap = total // devices
    flat_rows = probe_atoms.reshape(-1)
    owner = jnp.where(flat_rows >= 0, flat_rows // hslot, devices)
    positions = jnp.arange(total)
    order = jnp.argsort(owner * total + positions)
    sorted_owner = owner[order]
    starts = jnp.searchsorted(sorted_owner, jnp.arange(devices))
    within = positions - starts[jnp.minimum(sorted_owner, devices - 1)]
    bucket = jnp.where(sorted_owner < devices, sorted_owner * slot_cap + within, devices * slot_cap)
    source_pos = (
        jnp.full((devices * slot_cap,), total, jnp.int32).at[bucket].set(order, mode="drop")
    )
    padded_rows = jnp.concatenate([flat_rows, jnp.full((1,), -1, jnp.int32)])
    picked_rows = padded_rows[source_pos]
    request_rows = jnp.where(picked_rows >= 0, picked_rows % hslot, -1).reshape(
        1, devices, slot_cap
    )
    dummy = jnp.array([[1.0], [0.0], [0.0]], jnp.float32)
    padded_off = jnp.concatenate([offsets.reshape(3, total), dummy], axis=1)
    request_off = padded_off[:, source_pos].reshape(3, devices, slot_cap)
    recv_off, recv_rows = (
        lax.all_to_all(request_off, ("slab", "dom"), split_axis=1, concat_axis=1, tiled=True),
        lax.all_to_all(request_rows, ("slab", "dom"), split_axis=1, concat_axis=1, tiled=True),
    )
    recv_rows = recv_rows.reshape(-1)
    source_slab = jnp.repeat(jnp.arange(devices) // n_dom, slot_cap)
    own_table = halo_lists[:, 0, :]
    local_atom = own_table[source_slab, jnp.maximum(recv_rows, 0)]
    item_live = (recv_rows >= 0).astype(jnp.float32)
    block_len = min(item_block, total)
    block_count = total // block_len
    atom_blocks = local_atom.reshape(block_count, block_len)
    live_blocks = item_live.reshape(block_count, block_len)
    off_blocks = recv_off.reshape(3, block_count, block_len).transpose(1, 0, 2)

    def item_sums(inputs):
        atoms, live, off = inputs
        radial, harmonic = geometry(off[:, None, :], radial_weights)
        gathered = atom_features[atoms].reshape(1, block_len, 25, channels)
        return contract_sums(gathered, harmonic, radial, live[None, :])

    partial_value = lax.map(item_sums, (atom_blocks, live_blocks, off_blocks)).reshape(
        devices, slot_cap, channels
    )
    back = lax.all_to_all(partial_value, ("slab", "dom"), split_axis=0, concat_axis=0, tiled=True)
    probe_of = jnp.where(source_pos < total, source_pos % probe_count, probe_count)
    summed = (
        jnp.zeros((probe_count, channels), jnp.float32)
        .at[probe_of]
        .add(back.reshape(-1, channels), mode="drop")
    )
    density, dsum = readout(summed, probe_weight, out_weight, density_cotangent)
    padded_ds = jnp.concatenate([dsum, jnp.zeros((1, channels), jnp.float32)], axis=0)
    ds_items = padded_ds[probe_of].reshape(devices, slot_cap, channels)
    ds_recv = lax.all_to_all(
        ds_items, ("slab", "dom"), split_axis=0, concat_axis=0, tiled=True
    ).reshape(block_count, block_len, channels)

    def item_grads(grads, inputs):
        atoms, live, off, ds_block = inputs
        radial, harmonic = geometry(off[:, None, :], radial_weights)
        weighted = (live[:, None] * ds_block)[None]
        rows = slot_grads(harmonic, radial, weighted).reshape(block_len, feature_len)
        return (grads.at[atoms].add(rows), None)

    atom_grads, unused = lax.scan(
        item_grads,
        jnp.zeros((atom_features.shape[0], feature_len), jnp.float32),
        (atom_blocks, live_blocks, off_blocks, ds_recv),
    )
    return (density, atom_grads)


def solution(mesh):
    return jax.shard_map(
        shards,
        mesh=mesh,
        in_specs=(
            P(("slab", "dom"), None),
            P(None, ("slab", "dom"), None),
            P(None, ("slab", "dom")),
            P(None, None, ("slab", "dom")),
            P(),
            P(),
            P(),
            P(("slab", "dom")),
        ),
        out_specs=(P(("slab", "dom")), P(("slab", "dom"), None)),
        check_vma=False,
    )
```

profile of v0, /device:TPU:0, one launch (start us, length us, event | category | flops | bytes accessed | tf_op | source)
XLA Modules:
  0.0 402.7 jit_solution(5138814613337710423)
XLA Ops:
  1.4 5.0 %sort.17 = (s32[2048]{0:T(1024)}, s32[2048]{0:T(1024)S(1)}) sort(s32[2048]{0:T(1024)S(1)} %get-tuple-element.411, s32[2048]{0:T(1024)S(1)} %iota.35), dimensions={0}, to_apply=%region_0.1 | sort | flops 22528 | bytes 32768 | tf_op jit(solution)/shard_map/jit(argsort)/sort | solution.py:114
  6.4 11.8 %gather_fusion.2 = s32[2048]{0:T(1024)S(1)} fusion(s32[2048]{0:T(1024)S(1)} %get-tuple-element.412, s32[2048]{0:T(1024)S(1)} %fusion.138), kind=kCustom, calls=%fused_computation.2 | custom fusion | bytes 24576 | tf_op jit(solution)/shard_map/gather | solution.py:115
  18.3 9.0 %while.52 = (s32[]{:T(128)}, u32[32]{0:T(128)S(1)}, u32[32]{0:T(128)S(1)}, s32[2048]{0:T(1024)S(1)}, s32[]{:T(128)}, /*index=5*/s32[]{:T(128)}, s32[]{}) while((s32[]{:T(128)}, u32[32]{0:T(128)S(1)}, u32[32]{0:T(128)S(1)}, s32[2048]{0:T(1024)S(1)}, s32[]{:T(128)}, /*index=5*/s32[]{:T(128)}, s32[]{}) %tuple.210), condition=%wide.region_2.3_spmd.clone, body=%wide.region_1.2_spmd.clone.sunk | while | flops 1444 | bytes 5740 | solution.py:116
  28.8 4.3 %compare_select_fusion.8 = (s32[2048,1]{0,1:T(1,128)S(1)}, s32[2048,1]{0,1:T(1,128)S(1)}) fusion(s32[]{:T(128)} %bitcast.145, s32[]{:T(128)} %bitcast.146, s32[]{:T(128)} %bitcast.147, s32[]{:T(128)} %bitcast.148, s32[]{:T(128)} %bitcast.149, s32[]{:T(128)} %bitcast.151, s32[]{:T(128)} %bitcast.150, s32[2048,1]{0,1:T(1,128)S(1)} %bitcast.807), kind=kLoop, calls=%fused_computation.292 | loop fusion | flops 30720 | bytes 24604 | tf_op jit(solution)/shard_map/gather | solution.py:117
  33.7 15.8 %select_select_fusion = s32[2048]{0:T(1024)S(1)} fusion(pred[2048]{0:T(1024)(128)(4,1)S(1)} %get-tuple-element.372, pred[2048]{0:T(1024)(128)(4,1)S(1)} %get-tuple-element.371, pred[2048]{0:T(1024)(128)(4,1)S(1)} %get-tuple-element.370, pred[2048]{0:T(1024)(128)(4,1)S(1)} %get-tuple-element.369, pred[2048]{0:T(1024)(128)(4,1)S(1)} %get-tuple-element.368, ...), kind=kLoop, calls=%fused_computation.324 | loop fusion | flops 51200 | bytes 67684 | tf_op jit(solution)/shard_map/gather | solution.py:117
  49.5 8.0 %scatter_custom_fusion.1 = s32[2048]{0:T(1024)S(1)} fusion(s32[2048]{0:T(1024)S(1)} %bitcast.813, s32[2048]{0:T(1024)S(1)} %get-tuple-element.306, s32[]{:T(128)} %constant.536.clone.1), kind=kCustom, calls=%fused_computation.331 | custom fusion | bytes 8196 | tf_op jit(solution)/shard_map/scatter | solution.py:120
  58.2 11.8 %gather_fusion.4 = s32[2048]{0:T(1024)S(1)} fusion(s32[2049]{0:T(1024)S(1)} %pad_add_fusion, s32[2048]{0:T(1024)S(1)} %get-tuple-element.471), kind=kCustom, calls=%fused_computation.4 | custom fusion | bytes 24576 | tf_op jit(solution)/shard_map/gather | solution.py:123
  70.8 7.3 %all-to-all-start.1 = ((s32[1,32,64]{2,0,1:T(1,128)}), s32[1,32,64]{2,0,1:T(1,128)S(1)}, u32[]{:S(2)}, u32[]{:S(2)}) async-start(s32[1,32,64]{2,0,1:T(1,128)} %compare_select_fusion.4), calls=%async_computation.1 | async-start | bytes 32768 | tf_op jit(solution)/shard_map/all_to_all | solution.py:132
  78.5 5.5 %gather_fusion.3 = f32[2048,3]{1,0:T(8,128)S(1)} fusion(f32[3,2049]{0,1:T(8,128)S(1)} %copy.31, s32[2048]{0:T(1024)S(1)} %get-tuple-element.471), kind=kCustom, calls=%fused_computation.3 | custom fusion | bytes 57344 | tf_op jit(solution)/shard_map/gather | solution.py:129
  85.2 5.8 %all-to-all-start = ((f32[32,1,192]{2,1,0:T(1,128)}), f32[32,1,192]{2,1,0:T(1,128)S(1)}, u32[]{:S(2)}, u32[]{:S(2)}) async-start(f32[32,1,192]{2,1,0:T(1,128)} %reshape.4724), calls=%async_computation | async-start | bytes 65536 | tf_op jit(solution)/shard_map/all_to_all | solution.py:131
  91.4 9.1 %gather_fusion.5 = s32[2048]{0:T(1024)S(1)} fusion(s32[8,8]{1,0:T(8,128)S(1)} %bitcast.786, s32[2048]{0:T(1024)S(1)} %bitcast.792), kind=kCustom, calls=%fused_computation.5 | custom fusion | bytes 32768 | tf_op jit(solution)/shard_map/gather | solution.py:137
  103.3 82.3 %while.50 = (s32[]{:T(128)}, f32[4,512,128]{2,1,0:T(8,128)}, f32[4,3,512]{2,0,1:T(4,128)S(1)}, f32[8,640]{1,0:T(8,128)S(1)}, s32[4,512]{1,0:T(4,128)}, /*index=5...) while((s32[]{:T(128)}, f32[4,512,128]{2,1,0:T(8,128)}, f32[4,3,512]{2,0,1:T(4,128)S(1)}, ...), condition=%wide.region_6.7_spmd, body=%wide.region_4.6_spmd.sunk | while | flops 36808216 | bytes 24268976 | solution.py:151
  104.0 4.1 %gather_fusion = bf16[512,3200]{1,0:T(8,128)(2,1)} fusion(bf16[128,3200]{1,0:T(8,128)(2,1)S(1)} %get-tuple-element.771, s32[1024]{0:T(1024)S(1)} %pad_clamp_fusion.4), kind=kCustom, calls=%fused_computation.1.clone.1 | custom fusion | bytes 6555648 | tf_op jit(solution)/shard_map/while/body/eval_jaxpr/gather | solution.py:148
  108.1 5.6 %copy.75 = bf16[512,3200]{0,1:T(8,128)(2,1)} copy(bf16[512,3200]{1,0:T(8,128)(2,1)} %gather_fusion) | data formatting | bytes 6553600 | tf_op jit(solution)/shard_map/while/body/eval_jaxpr/gather | solution.py:148
  114.0 1.5 multiply_reduce_fusion.8
  124.6 4.1 %gather_fusion = bf16[512,3200]{1,0:T(8,128)(2,1)} fusion(bf16[128,3200]{1,0:T(8,128)(2,1)S(1)} %get-tuple-element.771, s32[1024]{0:T(1024)S(1)} %pad_clamp_fusion.4), kind=kCustom, calls=%fused_computation.1.clone.1 | custom fusion | bytes 6555648 | tf_op jit(solution)/shard_map/while/body/eval_jaxpr/gather | solution.py:148
  128.6 5.6 %copy.75 = bf16[512,3200]{0,1:T(8,128)(2,1)} copy(bf16[512,3200]{1,0:T(8,128)(2,1)} %gather_fusion) | data formatting | bytes 6553600 | tf_op jit(solution)/shard_map/while/body/eval_jaxpr/gather | solution.py:148
  134.5 1.5 multiply_reduce_fusion.8
  145.1 4.1 %gather_fusion = bf16[512,3200]{1,0:T(8,128)(2,1)} fusion(bf16[128,3200]{1,0:T(8,128)(2,1)S(1)} %get-tuple-element.771, s32[1024]{0:T(1024)S(1)} %pad_clamp_fusion.4), kind=kCustom, calls=%fused_computation.1.clone.1 | custom fusion | bytes 6555648 | tf_op jit(solution)/shard_map/while/body/eval_jaxpr/gather | solution.py:148
  149.2 5.6 %copy.75 = bf16[512,3200]{0,1:T(8,128)(2,1)} copy(bf16[512,3200]{1,0:T(8,128)(2,1)} %gather_fusion) | data formatting | bytes 6553600 | tf_op jit(solution)/shard_map/while/body/eval_jaxpr/gather | solution.py:148
  155.1 1.5 multiply_reduce_fusion.8
  158.2 1.4 multiply_reduce_fusion.9
  165.7 4.1 %gather_fusion = bf16[512,3200]{1,0:T(8,128)(2,1)} fusion(bf16[128,3200]{1,0:T(8,128)(2,1)S(1)} %get-tuple-element.771, s32[1024]{0:T(1024)S(1)} %pad_clamp_fusion.4), kind=kCustom, calls=%fused_computation.1.clone.1 | custom fusion | bytes 6555648 | tf_op jit(solution)/shard_map/while/body/eval_jaxpr/gather | solution.py:148
  169.8 5.6 %copy.75 = bf16[512,3200]{0,1:T(8,128)(2,1)} copy(bf16[512,3200]{1,0:T(8,128)(2,1)} %gather_fusion) | data formatting | bytes 6553600 | tf_op jit(solution)/shard_map/while/body/eval_jaxpr/gather | solution.py:148
  175.7 1.5 multiply_reduce_fusion.8
  178.8 1.4 multiply_reduce_fusion.9
  185.6 32.1 %all_to_all.20 = f32[32,64,128]{2,1,0:T(8,128)S(1)} all-to-all(f32[32,64,128]{2,1,0:T(8,128)} %bitcast.794), channel_id=1, replica_groups=mesh['slab'=8,'dom'=4] {'slab','dom'}, dimensions={0} | all-to-all | bytes 2097152 | tf_op jit(solution)/shard_map/all_to_all | solution.py:154
  217.6 11.6 %scatter_custom_fusion.2 = f32[256,128]{1,0:T(8,128)S(1)} fusion(s32[2048]{0:T(1024)} %get-tuple-element.470, f32[2048,128]{1,0:T(8,128)S(1)} %bitcast.795, f32[]{:T(128)} %constant.535.clone.1), kind=kCustom, calls=%fused_computation.258 | custom fusion | flops 262144 | bytes 131584 | tf_op jit(solution)/shard_map/scatter-add | solution.py:159
  229.9 7.6 %gather_fusion.6 = f32[2048,128]{1,0:T(8,128)} fusion(f32[257,128]{1,0:T(8,128)S(1)} %concatenate.56, s32[2048]{0:T(1024)S(1)} %copy-done.12), kind=kCustom, calls=%fused_computation.6 | custom fusion | bytes 2105344 | tf_op jit(solution)/shard_map/gather | solution.py:163
  237.5 3.7 all-to-all-start.3
  242.1 25.4 %all-to-all-done.3 = f32[32,64,128]{2,1,0:T(8,128)} async-done(((f32[32,64,128]{2,1,0:T(8,128)}), f32[32,64,128]{2,1,0:T(8,128)}, u32[]{:S(2)}, u32[]{:S(2)}) %all-to-all-start.3) | async-done | bytes 1048608 | tf_op jit(solution)/shard_map/all_to_all | solution.py:164
  267.6 133.9 %while.51 = (s32[]{:T(128)}, f32[128,3200]{1,0:T(8,128)S(1)}, s32[4,512]{1,0:T(4,128)}, f32[4,512]{1,0:T(4,128)}, f32[4,512,128]{2,1,0:T(8,128)}, /*index=5*/f32...) while((s32[]{:T(128)}, f32[128,3200]{1,0:T(8,128)S(1)}, s32[4,512]{1,0:T(4,128)}, f32[4,512]{1,0:T(4,128)}, ...), condition=%wide.region_11.12_spmd, body=%wide.region_8.11_spmd.sunk | while | flops 35300888 | bytes 48357748 | solution.py:175
  277.2 1.5 multiply_dynamic-update-slice_fusion.10
  278.7 1.7 multiply_dynamic-update-slice_fusion.11
  280.4 8.2 %copy.82 = f32[512,3200]{1,0:T(8,128)} copy(f32[512,3200]{0,1:T(8,128)} %bitcast.785) | data formatting | bytes 13107200 | tf_op jit(solution)/shard_map/while/body/eval_jaxpr/reshape | solution.py:172
  288.6 12.4 %scatter_fusion = f32[128,3200]{1,0:T(8,128)S(1)} fusion(f32[128,3200]{1,0:T(8,128)S(1)} %get-tuple-element.783, s32[512]{0:T(512)S(1)} %bitcast.801, f32[512,3200]{1,0:T(8,128)} %copy.82), kind=kCustom, calls=%fused_computation.7.clone.1 | custom fusion | flops 1638400 | bytes 19662848 | tf_op jit(solution)/shard_map/while/body/eval_jaxpr/scatter-add | solution.py:173
  310.6 1.5 multiply_dynamic-update-slice_fusion.10
  312.2 1.7 multiply_dynamic-update-slice_fusion.11
  313.9 8.2 %copy.82 = f32[512,3200]{1,0:T(8,128)} copy(f32[512,3200]{0,1:T(8,128)} %bitcast.785) | data formatting | bytes 13107200 | tf_op jit(solution)/shard_map/while/body/eval_jaxpr/reshape | solution.py:172
  322.1 12.4 %scatter_fusion = f32[128,3200]{1,0:T(8,128)S(1)} fusion(f32[128,3200]{1,0:T(8,128)S(1)} %get-tuple-element.783, s32[512]{0:T(512)S(1)} %bitcast.801, f32[512,3200]{1,0:T(8,128)} %copy.82), kind=kCustom, calls=%fused_computation.7.clone.1 | custom fusion | flops 1638400 | bytes 19662848 | tf_op jit(solution)/shard_map/while/body/eval_jaxpr/scatter-add | solution.py:173
  344.1 1.5 multiply_dynamic-update-slice_fusion.10
  345.6 1.7 multiply_dynamic-update-slice_fusion.11
  347.4 8.2 %copy.82 = f32[512,3200]{1,0:T(8,128)} copy(f32[512,3200]{0,1:T(8,128)} %bitcast.785) | data formatting | bytes 13107200 | tf_op jit(solution)/shard_map/while/body/eval_jaxpr/reshape | solution.py:172
  355.6 12.4 %scatter_fusion = f32[128,3200]{1,0:T(8,128)S(1)} fusion(f32[128,3200]{1,0:T(8,128)S(1)} %get-tuple-element.783, s32[512]{0:T(512)S(1)} %bitcast.801, f32[512,3200]{1,0:T(8,128)} %copy.82), kind=kCustom, calls=%fused_computation.7.clone.1 | custom fusion | flops 1638400 | bytes 19662848 | tf_op jit(solution)/shard_map/while/body/eval_jaxpr/scatter-add | solution.py:173
  377.6 1.5 multiply_dynamic-update-slice_fusion.10
  379.1 1.7 multiply_dynamic-update-slice_fusion.11
  380.9 8.2 %copy.82 = f32[512,3200]{1,0:T(8,128)} copy(f32[512,3200]{0,1:T(8,128)} %bitcast.785) | data formatting | bytes 13107200 | tf_op jit(solution)/shard_map/while/body/eval_jaxpr/reshape | solution.py:172
  389.1 12.4 %scatter_fusion = f32[128,3200]{1,0:T(8,128)S(1)} fusion(f32[128,3200]{1,0:T(8,128)S(1)} %get-tuple-element.783, s32[512]{0:T(512)S(1)} %bitcast.801, f32[512,3200]{1,0:T(8,128)} %copy.82), kind=kCustom, calls=%fused_computation.7.clone.1 | custom fusion | flops 1638400 | bytes 19662848 | tf_op jit(solution)/shard_map/while/body/eval_jaxpr/scatter-add | solution.py:173
  (378 shorter events, 92.2 us)
Async XLA Ops:
  0.6 228.6 %copy-start = (f32[128,128]{1,0:T(8,128)S(1)}, f32[128,128]{1,0:T(8,128)}, u32[]{:S(2)}) copy-start(f32[128,128]{1,0:T(8,128)} %param.20) | copy-start | bytes 196612
  58.2 19.9 %copy-start.13 = (f32[3,8,256]{2,1,0:T(8,128)S(1)}, f32[3,8,256]{2,1,0:T(8,128)}, u32[]{:S(2)}) copy-start(f32[3,8,256]{2,1,0:T(8,128)} %param.18) | copy-start | bytes 73732
  58.2 19.9 %copy-start.14 = (f32[3,1]{1,0:T(4,128)S(1)}, f32[3,1]{1,0:T(4,128)}, u32[]{:S(2)}) copy-start(f32[3,1]{1,0:T(4,128)} %constant.555.clone) | copy-start | bytes 40
  70.0 21.3 %copy-start.3 = (s32[8,1,8]{2,1,0:T(1,128)S(1)}, s32[8,1,8]{2,1,0:T(1,128)}, u32[]{:S(2)}) copy-start(s32[8,1,8]{2,1,0:T(1,128)} %param.16) | copy-start | bytes 772
  70.8 14.5 %all-to-all-start.1 = ((s32[1,32,64]{2,0,1:T(1,128)}), s32[1,32,64]{2,0,1:T(1,128)S(1)}, u32[]{:S(2)}, u32[]{:S(2)}) async-start(s32[1,32,64]{2,0,1:T(1,128)} %compare_select_fusion.4), calls=%async_computation.1 | async-start | bytes 32768 | tf_op jit(solution)/shard_map/all_to_all | solution.py:132
  85.2 16.5 %all-to-all-start = ((f32[32,1,192]{2,1,0:T(1,128)}), f32[32,1,192]{2,1,0:T(1,128)S(1)}, u32[]{:S(2)}, u32[]{:S(2)}) async-start(f32[32,1,192]{2,1,0:T(1,128)} %reshape.4724), calls=%async_computation | async-start | bytes 65536 | tf_op jit(solution)/shard_map/all_to_all | solution.py:131
  91.3 11.9 %copy-start.2 = (bf16[128,3200]{1,0:T(8,128)(2,1)S(1)}, bf16[128,3200]{1,0:T(8,128)(2,1)}, u32[]{:S(2)}) copy-start(bf16[128,3200]{1,0:T(8,128)(2,1)} %param.15) | copy-start | bytes 2457604
  91.4 11.9 %copy-start.6 = (f32[8,640]{1,0:T(8,128)S(1)}, f32[8,640]{1,0:T(8,128)}, u32[]{:S(2)}) copy-start(f32[8,640]{1,0:T(8,128)} %param.19) | copy-start | bytes 61444
  185.6 44.0 %copy-start.15 = (f32[256]{0:T(256)S(1)}, f32[256]{0:T(256)}, u32[]{:S(2)}) copy-start(f32[256]{0:T(256)} %param.22) | copy-start | bytes 3076
  185.6 44.0 %copy-start.16 = (f32[128]{0:T(128)S(1)}, f32[128]{0:T(128)}, u32[]{:S(2)}) copy-start(f32[128]{0:T(128)} %param.21) | copy-start | bytes 1540
  185.6 44.3 %copy-start.12 = (s32[2048]{0:T(1024)S(1)}, s32[2048]{0:T(1024)}, u32[]{:S(2)}) copy-start(s32[2048]{0:T(1024)} %get-tuple-element.469) | copy-start | bytes 24580
  237.5 30.0 %all-to-all-start.3 = ((f32[32,64,128]{2,1,0:T(8,128)}), f32[32,64,128]{2,1,0:T(8,128)}, u32[]{:S(2)}, u32[]{:S(2)}) async-start(f32[32,64,128]{2,1,0:T(8,128)} %bitcast.164), calls=%async_computation.3 | async-start | bytes 2097152 | tf_op jit(solution)/shard_map/all_to_all | solution.py:164
  267.6 2.7 copy-start.7
  267.6 2.7 copy-start.9
  273.9 3.3 copy-start.5
  274.8 3.9 copy-start.4
  280.4 8.2 %copy-start.11 = (s32[512,1]{0,1:T(1,128)S(1)}, s32[512,1]{0,1:T(1,128)}, u32[]{:S(2)}) copy-start(s32[512,1]{0,1:T(1,128)} %compare_select_fusion.24) | copy-start | bytes 6148 | tf_op jit(solution)/shard_map/while
  288.6 12.4 %copy-start.8 = (f32[8,640]{1,0:T(8,128)S(1)}, f32[8,640]{1,0:T(8,128)}, u32[]{:S(2)}) copy-start(f32[8,640]{1,0:T(8,128)} %copy-done.7) | copy-start | bytes 61444 | tf_op jit(solution)/shard_map/while
  288.6 12.5 %copy-start.10 = (f32[4,3,512]{2,0,1:T(4,128)S(1)}, f32[4,3,512]{2,0,1:T(4,128)}, u32[]{:S(2)}) copy-start(f32[4,3,512]{2,0,1:T(4,128)} %copy-done.9) | copy-start | bytes 73732 | tf_op jit(solution)/shard_map/while
  301.1 2.7 copy-start.7
  301.1 2.7 copy-start.9
  307.4 3.3 copy-start.5
  308.2 3.9 copy-start.4
  313.9 8.2 %copy-start.11 = (s32[512,1]{0,1:T(1,128)S(1)}, s32[512,1]{0,1:T(1,128)}, u32[]{:S(2)}) copy-start(s32[512,1]{0,1:T(1,128)} %compare_select_fusion.24) | copy-start | bytes 6148 | tf_op jit(solution)/shard_map/while
  322.1 12.4 %copy-start.8 = (f32[8,640]{1,0:T(8,128)S(1)}, f32[8,640]{1,0:T(8,128)}, u32[]{:S(2)}) copy-start(f32[8,640]{1,0:T(8,128)} %copy-done.7) | copy-start | bytes 61444 | tf_op jit(solution)/shard_map/while
  322.1 12.5 %copy-start.10 = (f32[4,3,512]{2,0,1:T(4,128)S(1)}, f32[4,3,512]{2,0,1:T(4,128)}, u32[]{:S(2)}) copy-start(f32[4,3,512]{2,0,1:T(4,128)} %copy-done.9) | copy-start | bytes 73732 | tf_op jit(solution)/shard_map/while
  334.6 2.7 copy-start.7
  334.6 2.7 copy-start.9
  340.8 3.3 copy-start.5
  341.7 3.9 copy-start.4
  347.4 8.2 %copy-start.11 = (s32[512,1]{0,1:T(1,128)S(1)}, s32[512,1]{0,1:T(1,128)}, u32[]{:S(2)}) copy-start(s32[512,1]{0,1:T(1,128)} %compare_select_fusion.24) | copy-start | bytes 6148 | tf_op jit(solution)/shard_map/while
  355.6 12.4 %copy-start.8 = (f32[8,640]{1,0:T(8,128)S(1)}, f32[8,640]{1,0:T(8,128)}, u32[]{:S(2)}) copy-start(f32[8,640]{1,0:T(8,128)} %copy-done.7) | copy-start | bytes 61444 | tf_op jit(solution)/shard_map/while
  355.6 12.5 %copy-start.10 = (f32[4,3,512]{2,0,1:T(4,128)S(1)}, f32[4,3,512]{2,0,1:T(4,128)}, u32[]{:S(2)}) copy-start(f32[4,3,512]{2,0,1:T(4,128)} %copy-done.9) | copy-start | bytes 73732 | tf_op jit(solution)/shard_map/while
  368.1 2.7 copy-start.7
  368.1 2.7 copy-start.9
  374.3 3.3 copy-start.5
  375.2 3.9 copy-start.4
  380.8 8.2 %copy-start.11 = (s32[512,1]{0,1:T(1,128)S(1)}, s32[512,1]{0,1:T(1,128)}, u32[]{:S(2)}) copy-start(s32[512,1]{0,1:T(1,128)} %compare_select_fusion.24) | copy-start | bytes 6148 | tf_op jit(solution)/shard_map/while
  389.1 12.4 %copy-start.8 = (f32[8,640]{1,0:T(8,128)S(1)}, f32[8,640]{1,0:T(8,128)}, u32[]{:S(2)}) copy-start(f32[8,640]{1,0:T(8,128)} %copy-done.7) | copy-start | bytes 61444 | tf_op jit(solution)/shard_map/while
  389.1 12.5 %copy-start.10 = (f32[4,3,512]{2,0,1:T(4,128)S(1)}, f32[4,3,512]{2,0,1:T(4,128)}, u32[]{:S(2)}) copy-start(f32[4,3,512]{2,0,1:T(4,128)} %copy-done.9) | copy-start | bytes 73732 | tf_op jit(solution)/shard_map/while
  401.5 1.2 copy-start.1
where the time goes:
time: 406 us; the launch traced here: 403 us
  local copies, waits for them, and re-layouts  158 us (39%)
  other arithmetic  155 us (38%)
  blocking collectives  32.1 us (8%)
  waiting for transfers between devices  25.4 us (6%)
  starting transfers between devices  16.9 us (4%)
  matrix products  11.9 us (3%)
    scatter-add x4, other arithmetic, item_grads(): return (grads.at[atoms].add(rows), None)  49.7 us
    while x48, other arithmetic  39 us
    gather x8, local copies, waits for them, and re-layouts, item_sums(): gathered = atom_features[atoms].reshape(1, block_len, 25, channels)  38.8 us
    reshape x4, local copies, waits for them, and re-layouts, item_grads(): slot_grads(harmonic, radial, weighted).reshape(block_len, feature_len)  32.9 us
    all_to_all x1, blocking collectives, shards(): lax.all_to_all(partial_value, ('slab', 'dom'), split_axis=0, concat_axis=...  32.1 us
    all_to_all x1, waiting for transfers between devices, shards(): lax.all_to_all(ds_items, ('slab', 'dom'), split_axis=0, concat_axis=0, ti...  25.4 us
    gather x3, other arithmetic, shards(): within = positions - starts[jnp.minimum(sorted_owner, devices - 1)]  20.7 us
    gather x2, local copies, waits for them, and re-layouts, shards(): picked_rows = padded_rows[source_pos]  11.9 us
  transfers between devices with their start and end apart: 3, of which 1 were waited for; matrix products, arithmetic and copies ran while one was open for 5% of the time, Pallas kernels for 0%

commit v1 on v0

v1 whole, which is shorter than its diff:
```python
import functools

import jax
import jax.numpy as jnp
from jax import lax
from jax.experimental import pallas as pl
from jax.experimental.pallas import tpu as pltpu
from jax.sharding import PartitionSpec as P

cutoff_radius = 4.0
COMPONENTS = 25
BF = jnp.bfloat16
F32 = jnp.float32
VMEM_LIMIT = 50 * 1024 * 1024


def iota(shape, dim):
    return lax.broadcasted_iota(jnp.int32, shape, dim)


def dot_nn(a, b):
    return lax.dot_general(a, b, (((1,), (0,)), ((), ())), preferred_element_type=F32)


def dot_nt(a, b):
    return lax.dot_general(a, b, (((1,), (1,)), ((), ())), preferred_element_type=F32)


def dot_tn(a, b):
    return lax.dot_general(a, b, (((0,), (0,)), ((), ())), preferred_element_type=F32)


def split(value):
    high = value.astype(BF)
    return high, (value - high.astype(F32)).astype(BF)


def harmonic_rows(xc, yc, zc):
    xsq = xc * xc
    ysq = yc * yc
    zsq = zc * zc
    return [
        0.28209479 * jnp.ones_like(xc),
        0.48860251 * yc,
        0.48860251 * zc,
        0.48860251 * xc,
        1.09254843 * xc * yc,
        1.09254843 * yc * zc,
        0.31539157 * (3.0 * zsq - 1.0),
        1.09254843 * xc * zc,
        0.54627422 * (xsq - ysq),
        0.59004359 * yc * (3.0 * xsq - ysq),
        2.89061144 * xc * yc * zc,
        0.4570458 * yc * (5.0 * zsq - 1.0),
        0.37317633 * zc * (5.0 * zsq - 3.0),
        0.4570458 * xc * (5.0 * zsq - 1.0),
        1.44530572 * zc * (xsq - ysq),
        0.59004359 * xc * (xsq - 3.0 * ysq),
        2.50334294 * xc * yc * (xsq - ysq),
        1.77013077 * yc * zc * (3.0 * xsq - ysq),
        0.9461747 * xc * yc * (7.0 * zsq - 1.0),
        0.66904654 * yc * zc * (7.0 * zsq - 3.0),
        0.10578555 * (35.0 * zsq * zsq - 30.0 * zsq + 3.0),
        0.66904654 * xc * zc * (7.0 * zsq - 3.0),
        0.47308735 * (xsq - ysq) * (7.0 * zsq - 1.0),
        1.77013077 * xc * zc * (xsq - 3.0 * ysq),
        0.62583574 * (xsq * (xsq - 3.0 * ysq) - ysq * (3.0 * xsq - ysq)),
    ]


def owner_onehot(halo, rows, atoms, hslot):
    n_slab = halo.shape[0]
    pick = (iota((rows, n_slab), 0) // hslot == iota((rows, n_slab), 1)).astype(BF)
    spread = dot_nn(pick, halo.astype(BF))
    mine = iota((rows, hslot), 0) % hslot == iota((rows, hslot), 1)
    column = jnp.sum(jnp.where(mine, spread, 0.0), axis=1, keepdims=True).astype(jnp.int32)
    return (iota((rows, atoms), 1) == column).astype(BF)


def pack_kernel(parts, h_ref, halo_ref, out_ref):
    n_slab, hslot = halo_ref.shape[0], halo_ref.shape[2]
    rows = n_slab * hslot
    onehot = owner_onehot(halo_ref[:, 0, :].astype(F32), rows, h_ref.shape[0], hslot)
    quarter = 128 // parts
    lane_part = iota((rows, 128), 1) // quarter
    groups = -(-COMPONENTS // parts)
    for group in range(groups):
        members = min(parts, COMPONENTS - group * parts)
        chosen = dot_nn(onehot, h_ref[:, group * parts * 128 : (group * parts + members) * 128])
        blocks = []
        for part in range(parts):
            total = jnp.zeros((rows, 128), F32)
            for i in range(members):
                source = chosen[:, i * 128 : (i + 1) * 128]
                shift = ((i - part) * quarter) % 128
                if shift:
                    source = pltpu.roll(source, shift, 1)
                total = jnp.where(lane_part == i, source, total)
            blocks.append(total.reshape(n_slab, hslot, 128))
        stacked = jnp.stack(blocks, axis=1).reshape(n_slab * parts * hslot, 128)
        out_ref[:, group * 128 : (group + 1) * 128] = stacked.astype(BF)


def unpack_kernel(parts, recv_ref, halo_ref, out_ref):
    n_slab, hslot = halo_ref.shape[0], halo_ref.shape[2]
    rows = n_slab * hslot
    onehot = owner_onehot(halo_ref[:, 0, :].astype(F32), rows, out_ref.shape[0], hslot)
    turned = onehot.astype(F32).T.astype(BF)
    quarter = 128 // parts
    lane_part = iota((rows, 128), 1) // quarter
    groups = -(-COMPONENTS // parts)
    for group in range(groups):
        members = min(parts, COMPONENTS - group * parts)
        got = recv_ref[:, group * 128 : (group + 1) * 128].astype(F32)
        got = got.reshape(n_slab, parts, hslot, 128)
        pieces = [got[:, part].reshape(rows, 128) for part in range(parts)]
        for i in range(members):
            total = jnp.zeros((rows, 128), F32)
            for part in range(parts):
                shift = ((part - i) * quarter) % 128
                source = pltpu.roll(pieces[part], shift, 1) if shift else pieces[part]
                total = jnp.where(lane_part == part, source, total)
            at = (group * parts + i) * 128
            out_ref[:, at : at + 128] = dot_nn(turned, total.astype(BF))


def basis_kernel(
    parts, channels, slots, probes, table,
    me_ref, *refs,
):
    blocks = refs[:parts]
    weight_ref = refs[parts]
    y_out, r_out, hot_out, turned_out, cot_out = refs[parts + 1 : parts + 6]
    geo, y_all, b_all, w_all = refs[parts + 6 :]
    k = pl.program_id(0)
    quarter = channels // parts
    orders = weight_ref.shape[0]

    @pl.when(k == 0)
    def _():
        me = me_ref[0]
        for j in range(parts):
            at = pl.multiple_of((me ^ j) * probes, 128)
            geo[:, pl.ds(at, probes)] = blocks[j][...]
        xo, yo, zo = (geo[i * slots : (i + 1) * slots, :] for i in range(3))
        length = jnp.sqrt(xo * xo + yo * yo + zo * zo)
        angle = jnp.pi * length / cutoff_radius
        sine, cosine = jnp.sin(angle), jnp.cos(angle)
        scale = (2.0 / cutoff_radius) ** 0.5 * (0.5 * (cosine + 1.0)) / length
        before, now = jnp.zeros_like(sine), sine
        high, low = [], []
        for _n in range(orders):
            one, two = split(now * scale)
            high.append(one.astype(F32))
            low.append(two.astype(F32))
            before, now = now, 2.0 * cosine * now - before
        size = orders * slots
        top = jnp.concatenate(high, axis=0).astype(BF)
        b_all[0:size, :] = top
        b_all[size : 2 * size, :] = top
        b_all[2 * size : 3 * size, :] = jnp.concatenate(low, axis=0).astype(BF)
        y_all[...] = jnp.zeros_like(y_all)
        unit = (xo / length, yo / length, zo / length)
        for index, row in enumerate(harmonic_rows(*unit)):
            row = row.astype(BF).astype(F32)
            for slot in range(slots):
                y_all[slot * 32 + index : slot * 32 + index + 1, :] = row[slot : slot + 1, :]
        cot_out[...] = geo[4 * slots : 5 * slots, :]
        weights = weight_ref[...]
        w_high, w_low = split(weights)
        w_high, w_low = w_high.astype(F32), w_low.astype(F32)
        spread = []
        for source in (w_high, w_low, w_high):
            for n in range(orders):
                spread.append(jnp.broadcast_to(source[n : n + 1, :], (slots, 5 * channels)))
        spread = jnp.concatenate(spread, axis=0).astype(BF)
        row = iota((5 * quarter, 5 * channels), 0)
        wanted = row // quarter * channels + me * quarter + row % quarter
        choose = (iota((5 * quarter, 5 * channels), 1) == wanted).astype(BF)
        w_all[...] = dot_nt(choose, spread)

    lane = iota(w_all.shape, 1)
    mine = jnp.where(lane % slots == k, w_all[...], 0.0).astype(BF)
    r_out[0] = dot_nn(mine, b_all[...])
    y_out[0] = y_all[pl.ds(pl.multiple_of(k * 32, 32), 32), :]
    atoms = geo[pl.ds(3 * slots + k, 1), :].astype(jnp.int32)
    hot = (iota((table, parts * probes), 0) == atoms).astype(F32)
    hot_out[0] = hot.astype(BF)
    turned_out[0] = hot.T.astype(BF)


def forward_kernel(quarter, h_ref, hot_ref, y_ref, r_ref, s_ref, turned, total):
    k = pl.program_id(0)

    @pl.when(k == 0)
    def _():
        turned[...] = h_ref[...].astype(F32).T.astype(BF)
        total[...] = jnp.zeros_like(total)

    width = total.shape[1]
    step = 256
    for at in range(0, width, step):
        lanes = slice(at, at + step)
        hot = hot_ref[0, :, lanes]
        acc = total[:, lanes]
        for degree in range(5):
            first, last = degree * degree, (degree + 1) ** 2
            got = dot_nn(turned[first * quarter : last * quarter, :], hot)
            inner = got[0:quarter] * y_ref[0, first : first + 1, lanes]
            for m in range(1, last - first):
                inner = inner + (
                    got[m * quarter : (m + 1) * quarter]
                    * y_ref[0, first + m : first + m + 1, lanes]
                )
            acc = acc + inner * r_ref[0, degree * quarter : (degree + 1) * quarter, lanes]
        total[:, lanes] = acc

    @pl.when(k == pl.num_programs(0) - 1)
    def _():
        s_ref[...] = total[...].astype(BF)


def backward_kernel(
    parts, quarter, probes,
    me_ref, *refs,
):
    sums = refs[:parts]
    pw_ref, ow_ref, cot_ref, turned_ref, y_ref, r_ref = refs[parts : parts + 6]
    grads_ref, density_ref = refs[parts + 6 : parts + 8]
    s_all, ds, z, acc, dens = refs[parts + 8 :]
    k = pl.program_id(0)
    me = me_ref[0]
    channels = parts * quarter

    @pl.when(k == 0)
    def _():
        for j in range(parts):
            at = pl.multiple_of((me ^ j) * quarter, quarter)
            s_all[pl.ds(at, quarter), :] = sums[j][...].astype(F32)
        pw = pw_ref[...]
        p_high, p_low = split(pw)
        given = s_all[...].astype(BF)
        pre = dot_tn(p_high, given) + dot_tn(p_low, given)
        eye = iota((channels, channels), 0) == iota((channels, channels), 1)
        ow = jnp.sum(jnp.where(eye, ow_ref[...], 0.0), axis=1, keepdims=True)
        sigma = 1.0 / (1.0 + jnp.exp(-pre))
        dens[...] = jnp.sum(pre * sigma * ow, axis=0, keepdims=True)
        here = pl.multiple_of(me * probes, 128)
        density_ref[...] = dens[:, pl.ds(here, probes)]
        dpre = cot_ref[0:1, :] * ow * sigma * (1.0 + pre * (1.0 - sigma))
        d_high, d_low = split(dpre)
        own = pl.multiple_of(me * quarter, quarter)
        o_high, o_low = split(pw_ref[pl.ds(own, quarter), :])
        ds[...] = dot_nn(o_high, d_high) + dot_nn(o_high, d_low) + dot_nn(o_low, d_high)
        acc[...] = jnp.zeros_like(acc)

    for degree in range(5):
        first, last = degree * degree, (degree + 1) ** 2
        weighted = ds[...] * r_ref[0, degree * quarter : (degree + 1) * quarter, :]
        for m in range(first, last):
            z[m * quarter : (m + 1) * quarter, :] = (weighted * y_ref[0, m : m + 1, :]).astype(BF)
    acc[...] += dot_nn(z[...], turned_ref[0])

    @pl.when(k == pl.num_programs(0) - 1)
    def _():
        filled = (COMPONENTS * quarter) // 128 * 128
        grads_ref[:, 0:filled] = acc[0:filled, :].T.astype(BF)
        rest = acc[filled : COMPONENTS * quarter, :]
        space = grads_ref.shape[1] - COMPONENTS * quarter
        rest = jnp.concatenate([rest, jnp.zeros((space, rest.shape[1]), F32)], axis=0)
        grads_ref[:, filled:] = rest.T.astype(BF)


def whole(shape):
    return pl.BlockSpec(shape, lambda *_: (0,) * len(shape))


def spread_over(value, n_dom):
    blocks = {0: value}
    bit = n_dom // 2
    while bit:
        pairs = [(i, i ^ bit) for i in range(n_dom)]
        for j in list(blocks):
            blocks[j | bit] = lax.ppermute(blocks[j], "dom", pairs)
        bit //= 2
    return [blocks[j] for j in range(n_dom)]


def shards(
    atom_features,
    halo_lists,
    probe_atoms,
    offsets,
    radial_weights,
    probe_weight,
    out_weight,
    density_cotangent,
):
    n_slab = lax.axis_size("slab")
    n_dom = lax.axis_size("dom")
    atoms, feature_len = atom_features.shape
    channels = feature_len // COMPONENTS
    slots, probes = probe_atoms.shape
    hslot = halo_lists.shape[2]
    table = n_slab * n_dom * hslot
    quarter = channels // n_dom
    orders = radial_weights.shape[0]
    slab_probes = n_dom * probes
    packed = -(-COMPONENTS // n_dom) * 128
    me = lax.axis_index("dom").astype(jnp.int32).reshape(1)
    params = pltpu.CompilerParams(vmem_limit_bytes=VMEM_LIMIT)

    geometry = jnp.concatenate(
        [
            offsets.reshape(3 * slots, probes),
            probe_atoms.astype(F32),
            jnp.broadcast_to(density_cotangent[None, :], (slots, probes)),
        ],
        axis=0,
    )
    geo_blocks = spread_over(geometry, n_dom)

    send = pl.pallas_call(
        functools.partial(pack_kernel, n_dom),
        out_shape=jax.ShapeDtypeStruct((table, packed), BF),
        compiler_params=params,
        name="pack",
    )(atom_features, halo_lists)
    halo = lax.all_to_all(send, ("slab", "dom"), split_axis=0, concat_axis=0, tiled=True)

    y_all, r_all, hot, hot_turned, cot = pl.pallas_call(
        functools.partial(basis_kernel, n_dom, channels, slots, probes, table),
        grid_spec=pltpu.PrefetchScalarGridSpec(
            num_scalar_prefetch=1,
            grid=(slots,),
            in_specs=[whole(geometry.shape)] * n_dom + [whole(radial_weights.shape)],
            out_specs=[
                pl.BlockSpec((1, 32, slab_probes), lambda k, _: (k, 0, 0)),
                pl.BlockSpec((1, 5 * quarter, slab_probes), lambda k, _: (k, 0, 0)),
                pl.BlockSpec((1, table, slab_probes), lambda k, _: (k, 0, 0)),
                pl.BlockSpec((1, slab_probes, table), lambda k, _: (k, 0, 0)),
                whole((slots, slab_probes)),
            ],
            scratch_shapes=[
                pltpu.VMEM((5 * slots, slab_probes), F32),
                pltpu.VMEM((32 * slots, slab_probes), F32),
                pltpu.VMEM((3 * orders * slots, slab_probes), BF),
                pltpu.VMEM((5 * quarter, 3 * orders * slots), F32),
            ],
        ),
        out_shape=[
            jax.ShapeDtypeStruct((slots, 32, slab_probes), F32),
            jax.ShapeDtypeStruct((slots, 5 * quarter, slab_probes), F32),
            jax.ShapeDtypeStruct((slots, table, slab_probes), BF),
            jax.ShapeDtypeStruct((slots, slab_probes, table), BF),
            jax.ShapeDtypeStruct((slots, slab_probes), F32),
        ],
        compiler_params=params,
        name="basis",
    )(me, *geo_blocks, radial_weights)

    sums = pl.pallas_call(
        functools.partial(forward_kernel, quarter),
        grid=(slots,),
        in_specs=[
            whole((table, packed)),
            pl.BlockSpec((1, table, slab_probes), lambda k: (k, 0, 0)),
            pl.BlockSpec((1, 32, slab_probes), lambda k: (k, 0, 0)),
            pl.BlockSpec((1, 5 * quarter, slab_probes), lambda k: (k, 0, 0)),
        ],
        out_specs=whole((quarter, slab_probes)),
        out_shape=jax.ShapeDtypeStruct((quarter, slab_probes), BF),
        scratch_shapes=[
            pltpu.VMEM((packed * n_dom // 128 * quarter, table), BF),
            pltpu.VMEM((quarter, slab_probes), F32),
        ],
        compiler_params=params,
        name="forward",
    )(halo, hot, y_all, r_all)

    sum_blocks = spread_over(sums, n_dom)

    grads, density = pl.pallas_call(
        functools.partial(backward_kernel, n_dom, quarter, probes),
        grid_spec=pltpu.PrefetchScalarGridSpec(
            num_scalar_prefetch=1,
            grid=(slots,),
            in_specs=[whole((quarter, slab_probes))] * n_dom
            + [
                whole((channels, channels)),
                whole((1, channels)),
                whole((slots, slab_probes)),
                pl.BlockSpec((1, slab_probes, table), lambda k, _: (k, 0, 0)),
                pl.BlockSpec((1, 32, slab_probes), lambda k, _: (k, 0, 0)),
                pl.BlockSpec((1, 5 * quarter, slab_probes), lambda k, _: (k, 0, 0)),
            ],
            out_specs=[whole((table, packed)), whole((1, probes))],
            scratch_shapes=[
                pltpu.VMEM((channels, slab_probes), F32),
                pltpu.VMEM((quarter, slab_probes), F32),
                pltpu.VMEM((COMPONENTS * quarter, slab_probes), BF),
                pltpu.VMEM((COMPONENTS * quarter, table), F32),
                pltpu.VMEM((1, slab_probes), F32),
            ],
        ),
        out_shape=[
            jax.ShapeDtypeStruct((table, packed), BF),
            jax.ShapeDtypeStruct((1, probes), F32),
        ],
        compiler_params=params,
        name="backward",
    )(me, *sum_blocks, probe_weight, out_weight.reshape(1, channels), cot, hot_turned, y_all, r_all)

    back = lax.all_to_all(grads, ("slab", "dom"), split_axis=0, concat_axis=0, tiled=True)
    atom_grads = pl.pallas_call(
        functools.partial(unpack_kernel, n_dom),
        out_shape=jax.ShapeDtypeStruct((atoms, feature_len), F32),
        compiler_params=params,
        name="unpack",
    )(back, halo_lists)
    return (density.reshape(probes), atom_grads)


def solution(mesh):
    return jax.shard_map(
        shards,
        mesh=mesh,
        in_specs=(
            P(("slab", "dom"), None),
            P(None, ("slab", "dom"), None),
            P(None, ("slab", "dom")),
            P(None, None, ("slab", "dom")),
            P(),
            P(),
            P(),
            P(("slab", "dom")),
        ),
        out_specs=(P(("slab", "dom")), P(("slab", "dom"), None)),
        check_vma=False,
    )
```

time: 406 us -> 73.7 us (0.18)
  local copies, waits for them, and re-layouts: 158 us -> 3.24 us
  other arithmetic: 155 us -> 1.44 us
  Pallas kernels: 0 us -> 29.3 us
  waiting for transfers between devices: 25.4 us -> 9.88 us
  blocking collectives: 32.1 us -> 18.3 us
  matrix products: 11.9 us -> 0 us
  starting transfers between devices: 16.9 us -> 10.1 us
    gather x28 -> x0, local copies, waits for them, and re-layouts: 94.6 us -> none  [the longest x8 38.8 us: item_sums(): gathered = atom_features[atoms].reshape(1, block_len, 25, channels)]
    scatter-add x5 -> x0, other arithmetic: 61.3 us -> none  [the longest x4 49.7 us: item_grads(): return (grads.at[atoms].add(rows), None)]
    while x48 -> x0, other arithmetic: 39 us -> none
    reshape x8 -> x0, local copies, waits for them, and re-layouts: 34 us -> none  [the longest x4 32.9 us: item_grads(): slot_grads(harmonic, radial, weighted).reshape(block_len, feature_len)]
    pallas_call x0 -> x5, Pallas kernels: none -> 29.3 us  [the longest x1 9.84 us: shards(): pl.pallas_call(functools.partial(backward_kernel, n_dom, quarter, probes)...]
    all_to_all x3 -> x1, waiting for transfers between devices: 25.4 us -> 0.01 us  [shards(): lax.all_to_all(send, ('slab', 'dom'), split_axis=0, concat_axis=0, tiled=...]
    gather x21 -> x0, other arithmetic: 21.4 us -> none  [the longest x3 20.7 us: shards(): within = positions - starts[jnp.minimum(sorted_owner, devices - 1)]]
    all_to_all x1, blocking collectives: 32.1 us -> 18.3 us  [shards(): lax.all_to_all(grads, ('slab', 'dom'), split_axis=0, concat_axis=0, tiled...]
  transfers between devices with their start and end apart: 3 -> 7, of which waited for: 1 -> 4; matrix products, arithmetic and copies ran while one was open for 5% -> 3% of each run, Pallas kernels for 0% -> 10%
where the time goes in v1:
time: 73.7 us; the launch traced here: 72.9 us
  Pallas kernels  29.3 us (40%)
  blocking collectives  18.3 us (25%)
  starting transfers between devices  10.1 us (14%)
  waiting for transfers between devices  9.88 us (13%)
  local copies, waits for them, and re-layouts  3.24 us (4%)
  other arithmetic  1.44 us (2%)
    all_to_all x1, blocking collectives, shards(): lax.all_to_all(grads, ('slab', 'dom'), split_axis=0, concat_axis=0, tiled...  18.3 us
    ppermute x6, waiting for transfers between devices, spread_over(): blocks[j | bit] = lax.ppermute(blocks[j], 'dom', pairs)  9.87 us
    pallas_call x1, Pallas kernels, shards(): pl.pallas_call(functools.partial(backward_kernel, n_dom, quarter, probes)...  9.84 us
    pallas_call x1, Pallas kernels, shards(): pl.pallas_call(functools.partial(forward_kernel, quarter), grid=(slots,),...  9.03 us
    all_to_all x1, starting transfers between devices, shards(): lax.all_to_all(send, ('slab', 'dom'), split_axis=0, concat_axis=0, tiled=...  7.29 us
    pallas_call x1, Pallas kernels, shards(): pl.pallas_call(functools.partial(basis_kernel, n_dom, channels, slots, pr...  7.11 us
    ppermute x6, starting transfers between devices, spread_over(): blocks[j | bit] = lax.ppermute(blocks[j], 'dom', pairs)  2.77 us
    unnamed x12, local copies, waits for them, and re-layouts  2.56 us
  transfers between devices with their start and end apart: 7, of which 4 were waited for; matrix products, arithmetic and copies ran while one was open for 3% of the time, Pallas kernels for 10%

profile of v1, /device:TPU:0, one launch (start us, length us, event | category | flops | bytes accessed | tf_op | source)
XLA Modules:
  0.0 72.9 jit_solution(16522644794636918909)
XLA Ops:
  0.6 0.0 copy-start
  0.6 1.1 %copy-done = bf16[128,3200]{1,0:T(8,128)(2,1)S(1)} copy-done((bf16[128,3200]{1,0:T(8,128)(2,1)S(1)}, bf16[128,3200]{1,0:T(8,128)(2,1)}, u32[]{:S(2)}) %copy-start) | copy-done | bytes 819224
  1.8 0.0 copy-start.3
  1.8 0.7 copy-done.3
  2.5 1.5 %pack.1 = bf16[256,896]{1,0:T(8,128)(2,1)} custom-call(bf16[128,3200]{1,0:T(8,128)(2,1)S(1)} %copy-done, s32[8,1,8]{2,1,0:T(1,128)S(1)} %copy-done.3), custom_call_target="tpu_custom_call" | custom-call | tf_op jit(solution)/shard_map/pack/pallas_call | solution.py:323
  4.0 7.3 %all-to-all-start = ((bf16[32,8,896]{2,1,0:T(8,128)(2,1)}), bf16[32,8,896]{2,1,0:T(8,128)(2,1)S(1)}, u32[]{:S(2)}, u32[]{:S(2)}) async-start(bf16[32,8,896]{2,1,0:T(8,128)(2,1)} %bitcast.1), calls=%async_computation | async-start | bytes 917504 | tf_op jit(solution)/shard_map/all_to_all | solution.py:329
  11.3 0.7 convert_element_type.3
  12.0 0.7 broadcast_in_dim.2
  12.7 0.7 %pad_maximum_fusion.refs_0_ = f32[40,256]{1,0:T(8,128)S(1)} fusion(f32[8,256]{1,0:T(8,128)S(1)} %broadcast_in_dim.2, f32[8,256]{1,0:T(8,128)S(1)} %convert_element_type.3, f32[24,256]{1,0:T(8,128)} %bitcast.12), kind=kLoop, calls=%fused_computation | loop fusion | flops 20480 | bytes 81920 | tf_op jit(solution)/shard_map/concatenate | solution.py:313
  13.4 1.8 %collective-permute-start.1 = (f32[40,256]{1,0:T(8,128)S(1)}, f32[40,256]{1,0:T(8,128)S(1)}, u32[]{:S(2)}, u32[]{:S(2)}) collective-permute-start(f32[40,256]{1,0:T(8,128)S(1)} %pad_maximum_fusion.refs_0_), channel_id=1, source_target_pairs={{0,2},{1,3},{2,0},{3,1},{4,6},{5,7},{6,4},{7,5},{8,10},{9,11},{10,... | collective-permute-start | bytes 122888 | tf_op jit(solution)/shard_map/ppermute | solution.py:284
  15.2 0.0 collective-permute-start
  15.2 4.1 %collective-permute-done.1.refs_2_ = f32[40,256]{1,0:T(8,128)S(1)} collective-permute-done((f32[40,256]{1,0:T(8,128)S(1)}, f32[40,256]{1,0:T(8,128)S(1)}, u32[]{:S(2)}, u32[]{:S(2)}) %collective-permute-start.1) | collective-permute-done | bytes 40992 | tf_op jit(solution)/shard_map/ppermute | solution.py:284
  19.2 0.0 collective-permute-start.2
  19.2 0.0 collective-permute-done.refs_1_
  19.2 1.2 %collective-permute-done.2.refs_3_ = f32[40,256]{1,0:T(8,128)S(1)} collective-permute-done((f32[40,256]{1,0:T(8,128)S(1)}, f32[40,256]{1,0:T(8,128)S(1)}, u32[]{:S(2)}, u32[]{:S(2)}) %collective-permute-start.2) | collective-permute-done | bytes 40992 | tf_op jit(solution)/shard_map/ppermute | solution.py:284
  20.5 0.0 copy-start.2
  20.5 0.7 copy-done.2
  21.2 7.1 %basis.1 = (f32[8,32,1024]{2,1,0:T(8,128)S(1)}, f32[8,160,1024]{2,1,0:T(8,128)}, bf16[8,256,1024]{2,1,0:T(8,128)(2,1)}, bf16[8,1024,256]{2,1,0:T(8,128)(2,1)}, f32[8,1024]{1,0:T(8,128)S(1)}) custom-call(s32[1]{0:T(128)} %bitcast.me_ref, f32[40,256]{1,0:T(8,128)S(1)} %pad_maximum_fusion.refs_0_, f32[40,256]{1,0:T(8,128)S(1)} %collective-permute-done.refs_1_, ...), custom_call_target="tpu_custom_call" | custom-call | tf_op jit(solution)/shard_map/basis/pallas_call | solution.py:331
  28.3 0.0 all-to-all-done
  28.3 0.0 copy-start.1
  28.3 0.0 copy-start.5
  28.3 9.0 %forward.1.refs_0_ = bf16[32,1024]{1,0:T(8,128)(2,1)S(1)} custom-call(bf16[256,896]{1,0:T(8,128)(2,1)S(1)} %bitcast.9, bf16[8,256,1024]{2,1,0:T(8,128)(2,1)} %get-tuple-element.9.hot_ref, f32[8,32,1024]{2,1,0:T(8,128)S(1)} %get-tuple-element.10.y_ref.refs_8_, f32[8,160,1024]{2,1,0:T(8,128)} %get-tuple-element.11.r_ref.refs_9_), custom_call_target="tpu_custom_call" | custom-call | tf_op jit(solution)/shard_map/forward/pallas_call | solution.py:362
  37.3 1.0 %collective-permute-start.4 = (bf16[32,1024]{1,0:T(8,128)(2,1)S(1)}, bf16[32,1024]{1,0:T(8,128)(2,1)S(1)}, u32[]{:S(2)}, u32[]{:S(2)}) collective-permute-start(bf16[32,1024]{1,0:T(8,128)(2,1)S(1)} %forward.1.refs_0_), channel_id=1, source_target_pairs={{0,2},{1,3},{2,0},{3,1},{4,6},{5,7},{6,4},{7,5},{8,10},{9,11},{10,... | collective-permute-start | bytes 196616 | tf_op jit(solution)/shard_map/ppermute | solution.py:284
  38.3 0.0 collective-permute-start.3
  38.3 3.3 %collective-permute-done.4.refs_2_ = bf16[32,1024]{1,0:T(8,128)(2,1)S(1)} collective-permute-done((bf16[32,1024]{1,0:T(8,128)(2,1)S(1)}, bf16[32,1024]{1,0:T(8,128)(2,1)S(1)}, u32[]{:S(2)}, u32[]{:S(2)}) %collective-permute-start.4) | collective-permute-done | bytes 65568 | tf_op jit(solution)/shard_map/ppermute | solution.py:284
  41.7 0.0 collective-permute-start.5
  41.7 0.0 collective-permute-done.3.refs_1_
  41.7 1.2 %collective-permute-done.5.refs_3_ = bf16[32,1024]{1,0:T(8,128)(2,1)S(1)} collective-permute-done((bf16[32,1024]{1,0:T(8,128)(2,1)S(1)}, bf16[32,1024]{1,0:T(8,128)(2,1)S(1)}, u32[]{:S(2)}, u32[]{:S(2)}) %collective-permute-start.5) | collective-permute-done | bytes 65568 | tf_op jit(solution)/shard_map/ppermute | solution.py:284
  42.9 0.0 copy-done.1
  42.9 0.0 copy-done.5
  42.9 0.0 copy-start.4
  42.9 9.8 %backward.1 = (bf16[256,896]{1,0:T(8,128)(2,1)S(1)}, f32[1,256]{1,0:T(1,128)}) custom-call(s32[1]{0:T(128)} %bitcast.me_ref, bf16[32,1024]{1,0:T(8,128)(2,1)S(1)} %forward.1.refs_0_, bf16[32,1024]{1,0:T(8,128)(2,1)S(1)} %collective-permute-done.3.refs_1_, bf16[32,1024]{1,0:T(8,128)(2,1)S(1)} %collective-permute-done.4.refs_2_, ...), custom_call_target="tpu_custom_call" | custom-call | tf_op jit(solution)/shard_map/backward/pallas_call | solution.py:383
  52.8 18.3 %all_to_all.22 = bf16[32,8,896]{2,1,0:T(8,128)(2,1)S(1)} all-to-all(bf16[32,8,896]{2,1,0:T(8,128)(2,1)S(1)} %bitcast.10), channel_id=1, replica_groups=mesh['slab'=8,'dom'=4] {'slab','dom'}, dimensions={0} | all-to-all | bytes 917504 | tf_op jit(solution)/shard_map/all_to_all | solution.py:414
  71.1 0.0 copy-done.4
  71.1 1.9 %unpack.1 = f32[128,3200]{1,0:T(8,128)} custom-call(bf16[256,896]{1,0:T(8,128)(2,1)S(1)} %bitcast.8, s32[8,1,8]{2,1,0:T(1,128)S(1)} %copy-done.4), custom_call_target="tpu_custom_call" | custom-call | tf_op jit(solution)/shard_map/unpack/pallas_call | solution.py:415
Async XLA Ops:
  0.6 1.1 %copy-start = (bf16[128,3200]{1,0:T(8,128)(2,1)S(1)}, bf16[128,3200]{1,0:T(8,128)(2,1)}, u32[]{:S(2)}) copy-start(bf16[128,3200]{1,0:T(8,128)(2,1)} %h_ref.1) | copy-start | bytes 2457604
  1.8 0.7 copy-start.3
  4.0 24.3 %all-to-all-start = ((bf16[32,8,896]{2,1,0:T(8,128)(2,1)}), bf16[32,8,896]{2,1,0:T(8,128)(2,1)S(1)}, u32[]{:S(2)}, u32[]{:S(2)}) async-start(bf16[32,8,896]{2,1,0:T(8,128)(2,1)} %bitcast.1), calls=%async_computation | async-start | bytes 917504 | tf_op jit(solution)/shard_map/all_to_all | solution.py:329
  13.4 5.8 %collective-permute-start.1 = (f32[40,256]{1,0:T(8,128)S(1)}, f32[40,256]{1,0:T(8,128)S(1)}, u32[]{:S(2)}, u32[]{:S(2)}) collective-permute-start(f32[40,256]{1,0:T(8,128)S(1)} %pad_maximum_fusion.refs_0_), channel_id=1, source_target_pairs={{0,2},{1,3},{2,0},{3,1},{4,6},{5,7},{6,4},{7,5},{8,10},{9,11},{10,... | collective-permute-start | bytes 122888 | tf_op jit(solution)/shard_map/ppermute | solution.py:284
  15.2 4.1 %collective-permute-start = (f32[40,256]{1,0:T(8,128)S(1)}, f32[40,256]{1,0:T(8,128)S(1)}, u32[]{:S(2)}, u32[]{:S(2)}) collective-permute-start(f32[40,256]{1,0:T(8,128)S(1)} %pad_maximum_fusion.refs_0_), channel_id=1, source_target_pairs={{0,1},{1,0},{2,3},{3,2},{4,5},{5,4},{6,7},{7,6},{8,9},{9,8},{10,11... | collective-permute-start | bytes 122888 | tf_op jit(solution)/shard_map/ppermute | solution.py:284
  19.2 1.2 %collective-permute-start.2 = (f32[40,256]{1,0:T(8,128)S(1)}, f32[40,256]{1,0:T(8,128)S(1)}, u32[]{:S(2)}, u32[]{:S(2)}) collective-permute-start(f32[40,256]{1,0:T(8,128)S(1)} %collective-permute-done.1.refs_2_), channel_id=1, source_target_pairs={{0,1},{1,0},{2,3},{3,2},{4,5},{5,4},{6,7},{7,6},{8,9},{9,8},{10,11... | collective-permute-start | bytes 122888 | tf_op jit(solution)/shard_map/ppermute | solution.py:284
  20.5 0.7 copy-start.2
  28.3 14.6 %copy-start.1 = (f32[128,128]{1,0:T(8,128)S(1)}, f32[128,128]{1,0:T(8,128)}, u32[]{:S(2)}) copy-start(f32[128,128]{1,0:T(8,128)} %refs_4_.3) | copy-start | bytes 196612
  28.3 14.6 %copy-start.5 = (f32[128]{0:T(128)S(1)}, f32[128]{0:T(128)}, u32[]{:S(2)}) copy-start(f32[128]{0:T(128)} %param.14) | copy-start | bytes 1540
  37.3 4.3 %collective-permute-start.4 = (bf16[32,1024]{1,0:T(8,128)(2,1)S(1)}, bf16[32,1024]{1,0:T(8,128)(2,1)S(1)}, u32[]{:S(2)}, u32[]{:S(2)}) collective-permute-start(bf16[32,1024]{1,0:T(8,128)(2,1)S(1)} %forward.1.refs_0_), channel_id=1, source_target_pairs={{0,2},{1,3},{2,0},{3,1},{4,6},{5,7},{6,4},{7,5},{8,10},{9,11},{10,... | collective-permute-start | bytes 196616 | tf_op jit(solution)/shard_map/ppermute | solution.py:284
  38.3 3.3 %collective-permute-start.3 = (bf16[32,1024]{1,0:T(8,128)(2,1)S(1)}, bf16[32,1024]{1,0:T(8,128)(2,1)S(1)}, u32[]{:S(2)}, u32[]{:S(2)}) collective-permute-start(bf16[32,1024]{1,0:T(8,128)(2,1)S(1)} %forward.1.refs_0_), channel_id=1, source_target_pairs={{0,1},{1,0},{2,3},{3,2},{4,5},{5,4},{6,7},{7,6},{8,9},{9,8},{10,11... | collective-permute-start | bytes 196616 | tf_op jit(solution)/shard_map/ppermute | solution.py:284
  41.7 1.3 %collective-permute-start.5 = (bf16[32,1024]{1,0:T(8,128)(2,1)S(1)}, bf16[32,1024]{1,0:T(8,128)(2,1)S(1)}, u32[]{:S(2)}, u32[]{:S(2)}) collective-permute-start(bf16[32,1024]{1,0:T(8,128)(2,1)S(1)} %collective-permute-done.4.refs_2_), channel_id=1, source_target_pairs={{0,1},{1,0},{2,3},{3,2},{4,5},{5,4},{6,7},{7,6},{8,9},{9,8},{10,11... | collective-permute-start | bytes 196616 | tf_op jit(solution)/shard_map/ppermute | solution.py:284
  42.9 28.2 %copy-start.4 = (s32[8,1,8]{2,1,0:T(1,128)S(1)}, s32[8,1,8]{2,1,0:T(1,128)}, u32[]{:S(2)}) copy-start(s32[8,1,8]{2,1,0:T(1,128)} %halo_ref.3) | copy-start | bytes 772

commit v2 on v1

v2 whole, which is shorter than its diff:
```python
import functools

import jax
import jax.numpy as jnp
from jax import lax
from jax.experimental import pallas as pl
from jax.experimental.pallas import tpu as pltpu
from jax.sharding import PartitionSpec as P

cutoff_radius = 4.0
COMPONENTS = 25
BF = jnp.bfloat16
F32 = jnp.float32


def iota(shape, dim):
    return lax.broadcasted_iota(jnp.int32, shape, dim)


def dot_nn(a, b):
    return lax.dot_general(a, b, (((1,), (0,)), ((), ())), preferred_element_type=F32)


def dot_nt(a, b):
    return lax.dot_general(a, b, (((1,), (1,)), ((), ())), preferred_element_type=F32)


def dot_tn(a, b):
    return lax.dot_general(a, b, (((0,), (0,)), ((), ())), preferred_element_type=F32)


def split(value):
    high = value.astype(BF)
    return high, (value - high.astype(F32)).astype(BF)


def harmonic_rows(xc, yc, zc):
    xsq = xc * xc
    ysq = yc * yc
    zsq = zc * zc
    return [
        0.28209479 * jnp.ones_like(xc),
        0.48860251 * yc,
        0.48860251 * zc,
        0.48860251 * xc,
        1.09254843 * xc * yc,
        1.09254843 * yc * zc,
        0.31539157 * (3.0 * zsq - 1.0),
        1.09254843 * xc * zc,
        0.54627422 * (xsq - ysq),
        0.59004359 * yc * (3.0 * xsq - ysq),
        2.89061144 * xc * yc * zc,
        0.4570458 * yc * (5.0 * zsq - 1.0),
        0.37317633 * zc * (5.0 * zsq - 3.0),
        0.4570458 * xc * (5.0 * zsq - 1.0),
        1.44530572 * zc * (xsq - ysq),
        0.59004359 * xc * (xsq - 3.0 * ysq),
        2.50334294 * xc * yc * (xsq - ysq),
        1.77013077 * yc * zc * (3.0 * xsq - ysq),
        0.9461747 * xc * yc * (7.0 * zsq - 1.0),
        0.66904654 * yc * zc * (7.0 * zsq - 3.0),
        0.10578555 * (35.0 * zsq * zsq - 30.0 * zsq + 3.0),
        0.66904654 * xc * zc * (7.0 * zsq - 3.0),
        0.47308735 * (xsq - ysq) * (7.0 * zsq - 1.0),
        1.77013077 * xc * zc * (xsq - 3.0 * ysq),
        0.62583574 * (xsq * (xsq - 3.0 * ysq) - ysq * (3.0 * xsq - ysq)),
    ]


def owner_onehot(halo, rows, atoms, hslot):
    n_slab = halo.shape[0]
    pick = (iota((rows, n_slab), 0) // hslot == iota((rows, n_slab), 1)).astype(BF)
    spread = dot_nn(pick, halo.astype(BF))
    mine = iota((rows, hslot), 0) % hslot == iota((rows, hslot), 1)
    column = jnp.sum(jnp.where(mine, spread, 0.0), axis=1, keepdims=True).astype(jnp.int32)
    return (iota((rows, atoms), 1) == column).astype(BF)


def pack_kernel(
    parts,
    h_hbm, halo_hbm, off_hbm, atoms_hbm, cot_hbm,
    out_ref, geo_ref,
    h_ref, halo_ref, off_ref, atoms_ref, cot_ref, sems,
):
    groups = -(-COMPONENTS // parts)
    small = [(halo_hbm, halo_ref), (off_hbm, off_ref), (atoms_hbm, atoms_ref), (cot_hbm, cot_ref)]
    copies = [
        pltpu.make_async_copy(source, target, sems.at[i]) for i, (source, target) in enumerate(small)
    ]
    for group in range(groups):
        lanes = slice(group * parts * 128, min((group + 1) * parts, COMPONENTS) * 128)
        copies.append(
            pltpu.make_async_copy(h_hbm.at[:, lanes], h_ref.at[:, lanes], sems.at[4 + group])
        )
    for copy in copies:
        copy.start()
    for copy in copies[:4]:
        copy.wait()
    slots = atoms_ref.shape[0]
    for i in range(3):
        geo_ref[i * slots : (i + 1) * slots, :] = off_ref[i]
    geo_ref[3 * slots : 4 * slots, :] = atoms_ref[...].astype(F32)
    geo_ref[4 * slots : 5 * slots, :] = jnp.broadcast_to(cot_ref[...], atoms_ref.shape)
    n_slab, hslot = halo_ref.shape[0], halo_ref.shape[2]
    rows = n_slab * hslot
    onehot = owner_onehot(halo_ref[:, 0, :].astype(F32), rows, h_ref.shape[0], hslot)
    quarter = 128 // parts
    lane_part = iota((rows, 128), 1) // quarter
    for group in range(groups):
        copies[4 + group].wait()
        members = min(parts, COMPONENTS - group * parts)
        chosen = dot_nn(onehot, h_ref[:, group * parts * 128 : (group * parts + members) * 128])
        blocks = []
        for part in range(parts):
            total = jnp.zeros((rows, 128), F32)
            for i in range(members):
                source = chosen[:, i * 128 : (i + 1) * 128]
                shift = ((i - part) * quarter) % 128
                if shift:
                    source = pltpu.roll(source, shift, 1)
                total = jnp.where(lane_part == i, source, total)
            blocks.append(total.reshape(n_slab, hslot, 128))
        stacked = jnp.stack(blocks, axis=1).reshape(n_slab * parts * hslot, 128)
        out_ref[:, group * 128 : (group + 1) * 128] = stacked.astype(BF)


def unpack_kernel(parts, recv_ref, halo_ref, out_hbm, out_ref, sems):
    n_slab, hslot = halo_ref.shape[0], halo_ref.shape[2]
    rows = n_slab * hslot
    onehot = owner_onehot(halo_ref[:, 0, :].astype(F32), rows, out_ref.shape[0], hslot)
    turned = onehot.astype(F32).T.astype(BF)
    quarter = 128 // parts
    lane_part = iota((rows, 128), 1) // quarter
    groups = -(-COMPONENTS // parts)
    copies = []
    for group in range(groups):
        members = min(parts, COMPONENTS - group * parts)
        got = recv_ref[:, group * 128 : (group + 1) * 128].astype(F32)
        got = got.reshape(n_slab, parts, hslot, 128)
        pieces = [got[:, part].reshape(rows, 128) for part in range(parts)]
        for i in range(members):
            total = jnp.zeros((rows, 128), F32)
            for part in range(parts):
                shift = ((part - i) * quarter) % 128
                source = pltpu.roll(pieces[part], shift, 1) if shift else pieces[part]
                total = jnp.where(lane_part == part, source, total)
            at = (group * parts + i) * 128
            out_ref[:, at : at + 128] = dot_nn(turned, total.astype(BF))
        lanes = slice(group * parts * 128, (group * parts + members) * 128)
        copy = pltpu.make_async_copy(out_ref.at[:, lanes], out_hbm.at[:, lanes], sems.at[group])
        copy.start()
        copies.append(copy)
    for copy in copies:
        copy.wait()


def basis_kernel(
    parts, channels, slots, probes,
    me_ref, *refs,
):
    blocks = refs[:parts]
    weight_ref = refs[parts]
    y_all, cot_out, atoms_out, b_all, w_all, geo = refs[parts + 1 :]
    quarter = channels // parts
    orders = weight_ref.shape[0]
    me = me_ref[0]
    for j in range(parts):
        at = pl.multiple_of((me ^ j) * probes, 128)
        geo[:, pl.ds(at, probes)] = blocks[j][...]
    xo, yo, zo = (geo[i * slots : (i + 1) * slots, :] for i in range(3))
    length = jnp.sqrt(xo * xo + yo * yo + zo * zo)
    angle = jnp.pi * length / cutoff_radius
    sine, cosine = jnp.sin(angle), jnp.cos(angle)
    scale = (2.0 / cutoff_radius) ** 0.5 * (0.5 * (cosine + 1.0)) / length
    before, now = jnp.zeros_like(sine), sine
    high, low = [], []
    for _n in range(orders):
        one, two = split(now * scale)
        high.append(one.astype(F32))
        low.append(two.astype(F32))
        before, now = now, 2.0 * cosine * now - before
    size = orders * slots
    top = jnp.concatenate(high, axis=0).astype(BF)
    b_all[0:size, :] = top
    b_all[size : 2 * size, :] = top
    b_all[2 * size : 3 * size, :] = jnp.concatenate(low, axis=0).astype(BF)
    unit = (xo / length, yo / length, zo / length)
    for index, row in enumerate(harmonic_rows(*unit)):
        row = row.astype(BF).astype(F32)
        for slot in range(slots):
            y_all[slot, index : index + 1, :] = row[slot : slot + 1, :]
    cot_out[...] = geo[4 * slots : 5 * slots, :]
    atoms_out[...] = geo[3 * slots : 4 * slots, :].astype(jnp.int32)
    weights = weight_ref[...]
    w_high, w_low = split(weights)
    w_high, w_low = w_high.astype(F32), w_low.astype(F32)
    spread = []
    for source in (w_high, w_low, w_high):
        for n in range(orders):
            spread.append(jnp.broadcast_to(source[n : n + 1, :], (slots, 5 * channels)))
    spread = jnp.concatenate(spread, axis=0).astype(BF)
    row = iota((5 * quarter, 5 * channels), 0)
    wanted = row // quarter * channels + me * quarter + row % quarter
    choose = (iota((5 * quarter, 5 * channels), 1) == wanted).astype(BF)
    w_all[...] = dot_nt(choose, spread)


def radial(k, slots, w_ref, b_ref, lanes):
    weights = w_ref[...]
    mine = jnp.where(iota(weights.shape, 1) % slots == k, weights, 0.0).astype(BF)
    return dot_nn(mine, b_ref[:, lanes])


def onehot_of(k, atoms_ref, table, lanes):
    atoms = atoms_ref[k : k + 1, lanes]
    return (iota((table, atoms.shape[1]), 0) == atoms).astype(F32).astype(BF)


def forward_kernel(
    quarter, h_ref, y_ref, atoms_ref, b_ref, w_ref, s_ref, hot_ref, r_ref, turned, total
):
    slots, table = atoms_ref.shape[0], h_ref.shape[0]
    turned[...] = h_ref[...].astype(F32).T.astype(BF)
    total[...] = jnp.zeros_like(total)
    width = total.shape[1]
    step = 256

    for k in range(slots):
        for at in range(0, width, step):
            lanes = slice(at, at + step)
            hot = onehot_of(k, atoms_ref, table, lanes)
            rad = radial(k, slots, w_ref, b_ref, lanes)
            hot_ref[k, :, lanes] = hot
            r_ref[k, :, lanes] = rad
            got = dot_nn(turned[0 : COMPONENTS * quarter, :], hot)
            acc = total[:, lanes]
            for degree in range(5):
                first, last = degree * degree, (degree + 1) ** 2
                inner = got[first * quarter : (first + 1) * quarter] * y_ref[k, first : first + 1, lanes]
                for m in range(first + 1, last):
                    inner = inner + (
                        got[m * quarter : (m + 1) * quarter] * y_ref[k, m : m + 1, lanes]
                    )
                acc = acc + inner * rad[degree * quarter : (degree + 1) * quarter]
            total[:, lanes] = acc
    s_ref[...] = total[...].astype(BF)


def backward_kernel(
    parts, quarter, probes,
    me_ref, *refs,
):
    sums = refs[:parts]
    pw_ref, ow_ref, cot_ref, y_ref, hot_ref, r_ref = refs[parts : parts + 6]
    grads_ref, density_ref, s_all, ds, z, acc, dens = refs[parts + 6 :]
    slots = y_ref.shape[0]
    me = me_ref[0]
    channels = parts * quarter
    for j in range(parts):
        at = pl.multiple_of((me ^ j) * quarter, quarter)
        s_all[pl.ds(at, quarter), :] = sums[j][...].astype(F32)
    pw = pw_ref[...]
    p_high, p_low = split(pw)
    given = s_all[...].astype(BF)
    pre = dot_tn(p_high, given) + dot_tn(p_low, given)
    eye = iota((channels, channels), 0) == iota((channels, channels), 1)
    ow = jnp.sum(jnp.where(eye, ow_ref[...], 0.0), axis=1, keepdims=True)
    sigma = 1.0 / (1.0 + jnp.exp(-pre))
    dens[...] = jnp.sum(pre * sigma * ow, axis=0, keepdims=True)
    here = pl.multiple_of(me * probes, 128)
    density_ref[...] = dens[:, pl.ds(here, probes)]
    dpre = cot_ref[0:1, :] * ow * sigma * (1.0 + pre * (1.0 - sigma))
    d_high, d_low = split(dpre)
    own = pl.multiple_of(me * quarter, quarter)
    o_high, o_low = split(pw_ref[pl.ds(own, quarter), :])
    ds[...] = dot_nn(o_high, d_high) + dot_nn(o_high, d_low) + dot_nn(o_low, d_high)
    acc[...] = jnp.zeros_like(acc)

    for k in range(slots):
        for degree in range(5):
            first, last = degree * degree, (degree + 1) ** 2
            weighted = ds[...] * r_ref[k, degree * quarter : (degree + 1) * quarter, :]
            for m in range(first, last):
                z[m * quarter : (m + 1) * quarter, :] = (
                    weighted * y_ref[k, m : m + 1, :]
                ).astype(BF)
        acc[...] += dot_nt(z[...], hot_ref[k])

    filled = (COMPONENTS * quarter) // 128 * 128
    grads_ref[:, 0:filled] = acc[0:filled, :].T.astype(BF)
    rest = acc[filled : COMPONENTS * quarter, :]
    space = grads_ref.shape[1] - COMPONENTS * quarter
    rest = jnp.concatenate([rest, jnp.zeros((space, rest.shape[1]), F32)], axis=0)
    grads_ref[:, filled:] = rest.T.astype(BF)


def spread_over(value, n_dom):
    blocks = {0: value}
    bit = n_dom // 2
    while bit:
        pairs = [(i, i ^ bit) for i in range(n_dom)]
        for j in list(blocks):
            blocks[j | bit] = lax.ppermute(blocks[j], "dom", pairs)
        bit //= 2
    return [blocks[j] for j in range(n_dom)]


def shards(
    atom_features,
    halo_lists,
    probe_atoms,
    offsets,
    radial_weights,
    probe_weight,
    out_weight,
    density_cotangent,
):
    n_slab = lax.axis_size("slab")
    n_dom = lax.axis_size("dom")
    atoms, feature_len = atom_features.shape
    channels = feature_len // COMPONENTS
    slots, probes = probe_atoms.shape
    hslot = halo_lists.shape[2]
    table = n_slab * n_dom * hslot
    quarter = channels // n_dom
    orders = radial_weights.shape[0]
    slab_probes = n_dom * probes
    packed = -(-COMPONENTS // n_dom) * 128
    me = lax.axis_index("dom").astype(jnp.int32).reshape(1)
    groups = -(-COMPONENTS // n_dom)
    wide = pltpu.CompilerParams(vmem_limit_bytes=56 * 2**20)
    narrow = pltpu.CompilerParams(vmem_limit_bytes=(16 if table <= 256 else 56) * 2**20)
    vmem = pl.BlockSpec(memory_space=pltpu.VMEM)
    smem = pl.BlockSpec(memory_space=pltpu.SMEM)
    any_space = pl.BlockSpec(memory_space=pl.ANY)

    send, geometry = pl.pallas_call(
        functools.partial(pack_kernel, n_dom),
        in_specs=[any_space] * 5,
        out_specs=[vmem, vmem],
        out_shape=[
            jax.ShapeDtypeStruct((table, packed), BF),
            jax.ShapeDtypeStruct((5 * slots, probes), F32),
        ],
        scratch_shapes=[
            pltpu.VMEM(atom_features.shape, BF),
            pltpu.VMEM(halo_lists.shape, jnp.int32),
            pltpu.VMEM(offsets.shape, F32),
            pltpu.VMEM(probe_atoms.shape, jnp.int32),
            pltpu.VMEM((1, probes), F32),
            pltpu.SemaphoreType.DMA((4 + groups,)),
        ],
        compiler_params=wide,
        name="pack",
    )(atom_features, halo_lists, offsets, probe_atoms, density_cotangent.reshape(1, probes))
    geo_blocks = spread_over(geometry, n_dom)
    halo = lax.all_to_all(send, ("slab", "dom"), split_axis=0, concat_axis=0, tiled=True)

    y_all, cot, listed, basis, weights = pl.pallas_call(
        functools.partial(basis_kernel, n_dom, channels, slots, probes),
        in_specs=[smem] + [vmem] * (n_dom + 1),
        out_specs=[vmem] * 5,
        scratch_shapes=[
            pltpu.VMEM((5 * slots, slab_probes), F32),
        ],
        out_shape=[
            jax.ShapeDtypeStruct((slots, 32, slab_probes), F32),
            jax.ShapeDtypeStruct((slots, slab_probes), F32),
            jax.ShapeDtypeStruct((slots, slab_probes), jnp.int32),
            jax.ShapeDtypeStruct((3 * orders * slots, slab_probes), BF),
            jax.ShapeDtypeStruct((5 * quarter, 3 * orders * slots), F32),
        ],
        compiler_params=narrow,
        name="basis",
    )(me, *geo_blocks, radial_weights)

    sums, hot, r_all = pl.pallas_call(
        functools.partial(forward_kernel, quarter),
        in_specs=[vmem] * 5,
        out_specs=[vmem] * 3,
        out_shape=[
            jax.ShapeDtypeStruct((quarter, slab_probes), BF),
            jax.ShapeDtypeStruct((slots, table, slab_probes), BF),
            jax.ShapeDtypeStruct((slots, 5 * quarter, slab_probes), F32),
        ],
        scratch_shapes=[
            pltpu.VMEM((packed * n_dom // 128 * quarter, table), BF),
            pltpu.VMEM((quarter, slab_probes), F32),
        ],
        compiler_params=narrow,
        name="forward",
    )(halo, y_all, listed, basis, weights)

    sum_blocks = spread_over(sums, n_dom)

    grads, density = pl.pallas_call(
        functools.partial(backward_kernel, n_dom, quarter, probes),
        in_specs=[smem] + [vmem] * (n_dom + 6),
        out_specs=[vmem, vmem],
        scratch_shapes=[
            pltpu.VMEM((channels, slab_probes), F32),
            pltpu.VMEM((quarter, slab_probes), F32),
            pltpu.VMEM((COMPONENTS * quarter, slab_probes), BF),
            pltpu.VMEM((COMPONENTS * quarter, table), F32),
            pltpu.VMEM((1, slab_probes), F32),
        ],
        out_shape=[
            jax.ShapeDtypeStruct((table, packed), BF),
            jax.ShapeDtypeStruct((1, probes), F32),
        ],
        compiler_params=narrow,
        name="backward",
    )(
        me, *sum_blocks, probe_weight, out_weight.reshape(1, channels), cot, y_all,
        hot, r_all,
    )

    back = lax.all_to_all(grads, ("slab", "dom"), split_axis=0, concat_axis=0, tiled=True)
    atom_grads = pl.pallas_call(
        functools.partial(unpack_kernel, n_dom),
        in_specs=[vmem, vmem],
        out_specs=any_space,
        scratch_shapes=[
            pltpu.VMEM((atoms, feature_len), F32),
            pltpu.SemaphoreType.DMA((groups,)),
        ],
        out_shape=jax.ShapeDtypeStruct((atoms, feature_len), F32),
        compiler_params=narrow,
        name="unpack",
    )(back, halo_lists)
    return (density.reshape(probes), atom_grads)


def solution(mesh):
    return jax.shard_map(
        shards,
        mesh=mesh,
        in_specs=(
            P(("slab", "dom"), None),
            P(None, ("slab", "dom"), None),
            P(None, ("slab", "dom")),
            P(None, None, ("slab", "dom")),
            P(),
            P(),
            P(),
            P(("slab", "dom")),
        ),
        out_specs=(P(("slab", "dom")), P(("slab", "dom"), None)),
        check_vma=False,
    )
```

time: 73.7 us -> 62.3 us (0.85)
  Pallas kernels: 29.3 us -> 16.2 us
  waiting for transfers between devices: 9.88 us -> 14.8 us
  other arithmetic: 1.44 us -> 0 us
  blocking collectives: 18.3 us -> 17 us
    pallas_call x1, Pallas kernels: 7.11 us -> 0.8 us  [shards(): pl.pallas_call(functools.partial(basis_kernel, n_dom, channels, slots, pr...]
    pallas_call x1, Pallas kernels: 9.84 us -> 4.71 us  [shards(): pl.pallas_call(functools.partial(backward_kernel, n_dom, quarter, probes)...]
    all_to_all x1, waiting for transfers between devices: 0.01 us -> 4.96 us  [shards(): lax.all_to_all(send, ('slab', 'dom'), split_axis=0, concat_axis=0, tiled=...]
    pallas_call x3, Pallas kernels: 12.4 us -> 10.7 us  [the longest x1 5.37 us: shards(): pl.pallas_call(functools.partial(forward_kernel, quarter), in_specs=[vmem...]
    all_to_all x1, blocking collectives: 18.3 us -> 17 us  [shards(): lax.all_to_all(grads, ('slab', 'dom'), split_axis=0, concat_axis=0, tiled...]
    concatenate x1 -> x0, other arithmetic: 0.74 us -> none  [shards(): jnp.concatenate([offsets.reshape(3 * slots, probes), probe_atoms.astype(F...]
    unnamed x12 -> x10, local copies, waits for them, and re-layouts: 2.56 us -> 3 us
  transfers between devices with their start and end apart: 7 -> 7, of which waited for: 4 -> 5; matrix products, arithmetic and copies ran while one was open for 3% -> 0% of each run, Pallas kernels for 10% -> 1%
where the time goes in v2:
time: 62.3 us; the launch traced here: 61.9 us
  blocking collectives  17 us (27%)
  Pallas kernels  16.2 us (26%)
  waiting for transfers between devices  14.8 us (24%)
  starting transfers between devices  10.1 us (16%)
  local copies, waits for them, and re-layouts  3 us (5%)
  between operations  0.68 us (1%)
    all_to_all x1, blocking collectives, shards(): lax.all_to_all(grads, ('slab', 'dom'), split_axis=0, concat_axis=0, tiled...  17 us
    ppermute x6, waiting for transfers between devices, spread_over(): blocks[j | bit] = lax.ppermute(blocks[j], 'dom', pairs)  9.88 us
    all_to_all x1, starting transfers between devices, shards(): lax.all_to_all(send, ('slab', 'dom'), split_axis=0, concat_axis=0, tiled=...  7.3 us
    pallas_call x1, Pallas kernels, shards(): pl.pallas_call(functools.partial(forward_kernel, quarter), in_specs=[vmem...  5.37 us
    all_to_all x1, waiting for transfers between devices, shards(): lax.all_to_all(send, ('slab', 'dom'), split_axis=0, concat_axis=0, tiled=...  4.96 us
    pallas_call x1, Pallas kernels, shards(): pl.pallas_call(functools.partial(backward_kernel, n_dom, quarter, probes)...  4.71 us
    pallas_call x1, Pallas kernels, shards(): pl.pallas_call(functools.partial(pack_kernel, n_dom), in_specs=[any_space...  3.62 us
    unnamed x10, local copies, waits for them, and re-layouts  3 us
  transfers between devices with their start and end apart: 7, of which 5 were waited for; matrix products, arithmetic and copies ran while one was open for 0% of the time, Pallas kernels for 1%

profile of v2, /device:TPU:0, one launch (start us, length us, event | category | flops | bytes accessed | tf_op | source)
XLA Modules:
  0.0 61.9 jit_solution(4808651793917392438)
XLA Ops:
  0.6 3.6 %pack.1 = (bf16[256,896]{1,0:T(8,128)(2,1)}, f32[40,256]{1,0:T(8,128)}) custom-call(bf16[128,3200]{1,0:T(8,128)(2,1)} %h_hbm.1, s32[8,1,8]{2,1,0:T(1,128)} %halo_ref.1, f32[3,8,256]{2,1,0:T(8,128)} %off_hbm.1, s32[8,256]{1,0:T(8,128)} %atoms_hbm.1, f32[1,256]{1,0:T(1,128)} %bitcast.13), custom_call_target="tpu_custom_call" | custom-call | tf_op jit(solution)/shard_map/pack/pallas_call | solution.py:337
  4.3 7.3 %all-to-all-start = ((bf16[32,8,896]{2,1,0:T(8,128)(2,1)}), bf16[32,8,896]{2,1,0:T(8,128)(2,1)S(1)}, u32[]{:S(2)}, u32[]{:S(2)}) async-start(bf16[32,8,896]{2,1,0:T(8,128)(2,1)} %bitcast.12), calls=%async_computation | async-start | bytes 917504 | tf_op jit(solution)/shard_map/all_to_all | solution.py:357
  11.6 1.8 %collective-permute-start.1 = (f32[40,256]{1,0:T(8,128)}, f32[40,256]{1,0:T(8,128)S(1)}, u32[]{:S(2)}, u32[]{:S(2)}) collective-permute-start(f32[40,256]{1,0:T(8,128)} %get-tuple-element.15.refs_0_), channel_id=1, source_target_pairs={{0,2},{1,3},{2,0},{3,1},{4,6},{5,7},{6,4},{7,5},{8,10},{9,11},{10,... | collective-permute-start | bytes 122888 | tf_op jit(solution)/shard_map/ppermute | solution.py:303
  13.4 0.0 collective-permute-start
  13.4 4.0 %collective-permute-done.1.refs_2_ = f32[40,256]{1,0:T(8,128)S(1)} collective-permute-done((f32[40,256]{1,0:T(8,128)}, f32[40,256]{1,0:T(8,128)S(1)}, u32[]{:S(2)}, u32[]{:S(2)}) %collective-permute-start.1) | collective-permute-done | bytes 40992 | tf_op jit(solution)/shard_map/ppermute | solution.py:303
  17.4 0.0 collective-permute-start.2
  17.4 0.0 collective-permute-done.refs_1_
  17.4 1.2 %collective-permute-done.2.refs_3_ = f32[40,256]{1,0:T(8,128)S(1)} collective-permute-done((f32[40,256]{1,0:T(8,128)S(1)}, f32[40,256]{1,0:T(8,128)S(1)}, u32[]{:S(2)}, u32[]{:S(2)}) %collective-permute-start.2) | collective-permute-done | bytes 40992 | tf_op jit(solution)/shard_map/ppermute | solution.py:303
  18.6 0.0 copy-start.1
  18.7 0.8 %copy-done.1 = f32[40,256]{1,0:T(8,128)S(1)} copy-done((f32[40,256]{1,0:T(8,128)S(1)}, f32[40,256]{1,0:T(8,128)}, u32[]{:S(2)}) %copy-start.1) | copy-done | bytes 40984
  19.4 0.0 copy-start.2
  19.4 0.7 %copy-done.2 = f32[8,640]{1,0:T(8,128)S(1)} copy-done((f32[8,640]{1,0:T(8,128)S(1)}, f32[8,640]{1,0:T(8,128)}, u32[]{:S(2)}) %copy-start.2) | copy-done | bytes 20504
  20.2 0.8 %basis.1 = (f32[8,32,1024]{2,1,0:T(8,128)S(1)}, f32[8,1024]{1,0:T(8,128)S(1)}, s32[8,1024]{1,0:T(8,128)S(1)}, bf16[192,1024]{1,0:T(8,128)(2,1)S(1)}, f32[160,192]{1,0:T(8,128)S(1)}) custom-call(s32[1]{0:T(128)} %bitcast.me_ref, f32[40,256]{1,0:T(8,128)S(1)} %copy-done.1, f32[40,256]{1,0:T(8,128)S(1)} %collective-permute-done.refs_1_, ...), custom_call_target="tpu_custom_call" | custom-call | tf_op jit(solution)/shard_map/basis/pallas_call | solution.py:359
  21.0 5.0 %all-to-all-done = bf16[32,8,896]{2,1,0:T(8,128)(2,1)S(1)} async-done(((bf16[32,8,896]{2,1,0:T(8,128)(2,1)}), bf16[32,8,896]{2,1,0:T(8,128)(2,1)S(1)}, u32[]{:S(2)}, u32[]{:S(2)}) %all-to-all-start) | async-done | bytes 458784 | tf_op jit(solution)/shard_map/all_to_all | solution.py:357
  25.9 5.4 %forward.1 = (bf16[32,1024]{1,0:T(8,128)(2,1)S(1)}, bf16[8,256,1024]{2,1,0:T(8,128)(2,1)S(1)}, f32[8,160,1024]{2,1,0:T(8,128)S(1)}) custom-call(bf16[256,896]{1,0:T(8,128)(2,1)S(1)} %bitcast.8, f32[8,32,1024]{2,1,0:T(8,128)S(1)} %get-tuple-element.16.y_ref.refs_7_, s32[8,1024]{1,0:T(8,128)S(1)} %get-tuple-element.17.atoms_ref, ...), custom_call_target="tpu_custom_call" | custom-call | tf_op jit(solution)/shard_map/forward/pallas_call | solution.py:377
  31.3 0.8 %collective-permute-start.4 = (bf16[32,1024]{1,0:T(8,128)(2,1)S(1)}, bf16[32,1024]{1,0:T(8,128)(2,1)S(1)}, u32[]{:S(2)}, u32[]{:S(2)}) collective-permute-start(bf16[32,1024]{1,0:T(8,128)(2,1)S(1)} %get-tuple-element.20.refs_0_), channel_id=1, source_target_pairs={{0,2},{1,3},{2,0},{3,1},{4,6},{5,7},{6,4},{7,5},{8,10},{9,11},{10,... | collective-permute-start | bytes 196616 | tf_op jit(solution)/shard_map/ppermute | solution.py:303
  32.1 0.2 collective-permute-start.3
  32.3 3.4 %collective-permute-done.4.refs_2_ = bf16[32,1024]{1,0:T(8,128)(2,1)S(1)} collective-permute-done((bf16[32,1024]{1,0:T(8,128)(2,1)S(1)}, bf16[32,1024]{1,0:T(8,128)(2,1)S(1)}, u32[]{:S(2)}, u32[]{:S(2)}) %collective-permute-start.4) | collective-permute-done | bytes 65568 | tf_op jit(solution)/shard_map/ppermute | solution.py:303
  35.6 0.0 collective-permute-start.5
  35.6 0.0 collective-permute-done.3.refs_1_
  35.6 1.2 %collective-permute-done.5.refs_3_ = bf16[32,1024]{1,0:T(8,128)(2,1)S(1)} collective-permute-done((bf16[32,1024]{1,0:T(8,128)(2,1)S(1)}, bf16[32,1024]{1,0:T(8,128)(2,1)S(1)}, u32[]{:S(2)}, u32[]{:S(2)}) %collective-permute-start.5) | collective-permute-done | bytes 65568 | tf_op jit(solution)/shard_map/ppermute | solution.py:303
  36.9 0.0 copy-start
  36.9 0.8 %copy-done = f32[128,128]{1,0:T(8,128)S(1)} copy-done((f32[128,128]{1,0:T(8,128)S(1)}, f32[128,128]{1,0:T(8,128)}, u32[]{:S(2)}) %copy-start) | copy-done | bytes 65560
  37.7 0.0 copy-start.4
  37.7 0.7 %copy-done.4 = f32[128]{0:T(128)S(1)} copy-done((f32[128]{0:T(128)S(1)}, f32[128]{0:T(128)}, u32[]{:S(2)}) %copy-start.4) | copy-done | bytes 536
  38.4 0.0 copy-start.3
  38.4 4.7 %backward.1 = (bf16[256,896]{1,0:T(8,128)(2,1)S(1)}, f32[1,256]{1,0:T(1,128)}) custom-call(s32[1]{0:T(128)} %bitcast.me_ref, bf16[32,1024]{1,0:T(8,128)(2,1)S(1)} %get-tuple-element.20.refs_0_, bf16[32,1024]{1,0:T(8,128)(2,1)S(1)} %collective-permute-done.3.refs_1_, bf16[32,1024]{1,0:T(8,128)(2,1)S(1)} %collective-permute-done.4.refs_2_, ...), custom_call_target="tpu_custom_call" | custom-call | tf_op jit(solution)/shard_map/backward/pallas_call | solution.py:396
  43.1 17.0 %all_to_all.22 = bf16[32,8,896]{2,1,0:T(8,128)(2,1)S(1)} all-to-all(bf16[32,8,896]{2,1,0:T(8,128)(2,1)S(1)} %bitcast.10), channel_id=1, replica_groups=mesh['slab'=8,'dom'=4] {'slab','dom'}, dimensions={0} | all-to-all | bytes 917504 | tf_op jit(solution)/shard_map/all_to_all | solution.py:418
  60.2 0.0 copy-done.3
  60.2 1.7 %unpack.1 = f32[128,3200]{1,0:T(8,128)} custom-call(bf16[256,896]{1,0:T(8,128)(2,1)S(1)} %bitcast.9, s32[8,1,8]{2,1,0:T(1,128)S(1)} %copy-done.3), custom_call_target="tpu_custom_call" | custom-call | tf_op jit(solution)/shard_map/unpack/pallas_call | solution.py:419
Async XLA Ops:
  4.3 21.7 %all-to-all-start = ((bf16[32,8,896]{2,1,0:T(8,128)(2,1)}), bf16[32,8,896]{2,1,0:T(8,128)(2,1)S(1)}, u32[]{:S(2)}, u32[]{:S(2)}) async-start(bf16[32,8,896]{2,1,0:T(8,128)(2,1)} %bitcast.12), calls=%async_computation | async-start | bytes 917504 | tf_op jit(solution)/shard_map/all_to_all | solution.py:357
  11.6 5.9 %collective-permute-start.1 = (f32[40,256]{1,0:T(8,128)}, f32[40,256]{1,0:T(8,128)S(1)}, u32[]{:S(2)}, u32[]{:S(2)}) collective-permute-start(f32[40,256]{1,0:T(8,128)} %get-tuple-element.15.refs_0_), channel_id=1, source_target_pairs={{0,2},{1,3},{2,0},{3,1},{4,6},{5,7},{6,4},{7,5},{8,10},{9,11},{10,... | collective-permute-start | bytes 122888 | tf_op jit(solution)/shard_map/ppermute | solution.py:303
  13.4 4.0 %collective-permute-start = (f32[40,256]{1,0:T(8,128)}, f32[40,256]{1,0:T(8,128)S(1)}, u32[]{:S(2)}, u32[]{:S(2)}) collective-permute-start(f32[40,256]{1,0:T(8,128)} %get-tuple-element.15.refs_0_), channel_id=1, source_target_pairs={{0,1},{1,0},{2,3},{3,2},{4,5},{5,4},{6,7},{7,6},{8,9},{9,8},{10,11... | collective-permute-start | bytes 122888 | tf_op jit(solution)/shard_map/ppermute | solution.py:303
  17.4 1.2 %collective-permute-start.2 = (f32[40,256]{1,0:T(8,128)S(1)}, f32[40,256]{1,0:T(8,128)S(1)}, u32[]{:S(2)}, u32[]{:S(2)}) collective-permute-start(f32[40,256]{1,0:T(8,128)S(1)} %collective-permute-done.1.refs_2_), channel_id=1, source_target_pairs={{0,1},{1,0},{2,3},{3,2},{4,5},{5,4},{6,7},{7,6},{8,9},{9,8},{10,11... | collective-permute-start | bytes 122888 | tf_op jit(solution)/shard_map/ppermute | solution.py:303
  18.6 0.8 %copy-start.1 = (f32[40,256]{1,0:T(8,128)S(1)}, f32[40,256]{1,0:T(8,128)}, u32[]{:S(2)}) copy-start(f32[40,256]{1,0:T(8,128)} %get-tuple-element.15.refs_0_) | copy-start | bytes 122884
  19.4 0.7 %copy-start.2 = (f32[8,640]{1,0:T(8,128)S(1)}, f32[8,640]{1,0:T(8,128)}, u32[]{:S(2)}) copy-start(f32[8,640]{1,0:T(8,128)} %refs_4_.2) | copy-start | bytes 61444
  31.3 4.3 %collective-permute-start.4 = (bf16[32,1024]{1,0:T(8,128)(2,1)S(1)}, bf16[32,1024]{1,0:T(8,128)(2,1)S(1)}, u32[]{:S(2)}, u32[]{:S(2)}) collective-permute-start(bf16[32,1024]{1,0:T(8,128)(2,1)S(1)} %get-tuple-element.20.refs_0_), channel_id=1, source_target_pairs={{0,2},{1,3},{2,0},{3,1},{4,6},{5,7},{6,4},{7,5},{8,10},{9,11},{10,... | collective-permute-start | bytes 196616 | tf_op jit(solution)/shard_map/ppermute | solution.py:303
  32.1 3.5 %collective-permute-start.3 = (bf16[32,1024]{1,0:T(8,128)(2,1)S(1)}, bf16[32,1024]{1,0:T(8,128)(2,1)S(1)}, u32[]{:S(2)}, u32[]{:S(2)}) collective-permute-start(bf16[32,1024]{1,0:T(8,128)(2,1)S(1)} %get-tuple-element.20.refs_0_), channel_id=1, source_target_pairs={{0,1},{1,0},{2,3},{3,2},{4,5},{5,4},{6,7},{7,6},{8,9},{9,8},{10,11... | collective-permute-start | bytes 196616 | tf_op jit(solution)/shard_map/ppermute | solution.py:303
  35.6 1.3 %collective-permute-start.5 = (bf16[32,1024]{1,0:T(8,128)(2,1)S(1)}, bf16[32,1024]{1,0:T(8,128)(2,1)S(1)}, u32[]{:S(2)}, u32[]{:S(2)}) collective-permute-start(bf16[32,1024]{1,0:T(8,128)(2,1)S(1)} %collective-permute-done.4.refs_2_), channel_id=1, source_target_pairs={{0,1},{1,0},{2,3},{3,2},{4,5},{5,4},{6,7},{7,6},{8,9},{9,8},{10,11... | collective-permute-start | bytes 196616 | tf_op jit(solution)/shard_map/ppermute | solution.py:303
  36.9 0.8 %copy-start = (f32[128,128]{1,0:T(8,128)S(1)}, f32[128,128]{1,0:T(8,128)}, u32[]{:S(2)}) copy-start(f32[128,128]{1,0:T(8,128)} %refs_4_.3) | copy-start | bytes 196612
  37.7 0.7 %copy-start.4 = (f32[128]{0:T(128)S(1)}, f32[128]{0:T(128)}, u32[]{:S(2)}) copy-start(f32[128]{0:T(128)} %param.14) | copy-start | bytes 1540
  38.4 21.8 %copy-start.3 = (s32[8,1,8]{2,1,0:T(1,128)S(1)}, s32[8,1,8]{2,1,0:T(1,128)}, u32[]{:S(2)}) copy-start(s32[8,1,8]{2,1,0:T(1,128)} %halo_ref.1) | copy-start | bytes 772

commit v3 on v2

--- a/solution.py
+++ b/solution.py
@@ -83,31 +83,28 @@
     h_ref, halo_ref, off_ref, atoms_ref, cot_ref, sems,
 ):
     groups = -(-COMPONENTS // parts)
-    small = [(halo_hbm, halo_ref), (off_hbm, off_ref), (atoms_hbm, atoms_ref), (cot_hbm, cot_ref)]
+    pairs = [
+        (halo_hbm, halo_ref), (h_hbm, h_ref), (off_hbm, off_ref), (atoms_hbm, atoms_ref), (cot_hbm, cot_ref)
+    ]
     copies = [
-        pltpu.make_async_copy(source, target, sems.at[i]) for i, (source, target) in enumerate(small)
+        pltpu.make_async_copy(source, target, sems.at[i]) for i, (source, target) in enumerate(pairs)
     ]
-    for group in range(groups):
-        lanes = slice(group * parts * 128, min((group + 1) * parts, COMPONENTS) * 128)
-        copies.append(
-            pltpu.make_async_copy(h_hbm.at[:, lanes], h_ref.at[:, lanes], sems.at[4 + group])
-        )
     for copy in copies:
         copy.start()
-    for copy in copies[:4]:
+    copies[0].wait()
+    n_slab, hslot = halo_ref.shape[0], halo_ref.shape[2]
+    rows = n_slab * hslot
+    onehot = owner_onehot(halo_ref[:, 0, :].astype(F32), rows, h_ref.shape[0], hslot)
+    for copy in copies[1:]:
         copy.wait()
     slots = atoms_ref.shape[0]
     for i in range(3):
         geo_ref[i * slots : (i + 1) * slots, :] = off_ref[i]
     geo_ref[3 * slots : 4 * slots, :] = atoms_ref[...].astype(F32)
     geo_ref[4 * slots : 5 * slots, :] = jnp.broadcast_to(cot_ref[...], atoms_ref.shape)
-    n_slab, hslot = halo_ref.shape[0], halo_ref.shape[2]
-    rows = n_slab * hslot
-    onehot = owner_onehot(halo_ref[:, 0, :].astype(F32), rows, h_ref.shape[0], hslot)
     quarter = 128 // parts
     lane_part = iota((rows, 128), 1) // quarter
     for group in range(groups):
-        copies[4 + group].wait()
         members = min(parts, COMPONENTS - group * parts)
         chosen = dot_nn(onehot, h_ref[:, group * parts * 128 : (group * parts + members) * 128])
         blocks = []
@@ -124,11 +121,10 @@
         out_ref[:, group * 128 : (group + 1) * 128] = stacked.astype(BF)
 
 
-def unpack_kernel(parts, recv_ref, halo_ref, out_hbm, out_ref, sems):
-    n_slab, hslot = halo_ref.shape[0], halo_ref.shape[2]
-    rows = n_slab * hslot
-    onehot = owner_onehot(halo_ref[:, 0, :].astype(F32), rows, out_ref.shape[0], hslot)
-    turned = onehot.astype(F32).T.astype(BF)
+def unpack_kernel(parts, hslot, recv_ref, turned_ref, out_hbm, out_ref, sems):
+    turned = turned_ref[...]
+    rows = turned.shape[1]
+    n_slab = rows // hslot
     quarter = 128 // parts
     lane_part = iota((rows, 128), 1) // quarter
     groups = -(-COMPONENTS // parts)
@@ -155,14 +151,11 @@
 
 
 def basis_kernel(
-    parts, channels, slots, probes,
+    parts, orders, slots, probes,
     me_ref, *refs,
 ):
     blocks = refs[:parts]
-    weight_ref = refs[parts]
-    y_all, cot_out, atoms_out, b_all, w_all, geo = refs[parts + 1 :]
-    quarter = channels // parts
-    orders = weight_ref.shape[0]
+    y_all, cot_out, atoms_out, b_all, geo = refs[parts:]
     me = me_ref[0]
     for j in range(parts):
         at = pl.multiple_of((me ^ j) * probes, 128)
@@ -191,6 +184,15 @@
             y_all[slot, index : index + 1, :] = row[slot : slot + 1, :]
     cot_out[...] = geo[4 * slots : 5 * slots, :]
     atoms_out[...] = geo[3 * slots : 4 * slots, :].astype(jnp.int32)
+
+
+def prepare_kernel(
+    parts, channels, slots,
+    me_ref, weight_ref, pw_ref, ow_ref, halo_ref, w_all, pw_out, own_out, turned_out,
+):
+    quarter = channels // parts
+    orders = weight_ref.shape[0]
+    me = me_ref[0]
     weights = weight_ref[...]
     w_high, w_low = split(weights)
     w_high, w_low = w_high.astype(F32), w_low.astype(F32)
@@ -203,6 +205,17 @@
     wanted = row // quarter * channels + me * quarter + row % quarter
     choose = (iota((5 * quarter, 5 * channels), 1) == wanted).astype(BF)
     w_all[...] = dot_nt(choose, spread)
+    p_high, p_low = split(pw_ref[...].T)
+    pw_out[:, 0:channels] = p_high
+    pw_out[:, channels : 2 * channels] = p_low
+    own = pw_ref[pl.ds(pl.multiple_of(me * quarter, quarter), quarter), :]
+    eye = iota((channels, channels), 0) == iota((channels, channels), 1)
+    column = jnp.sum(jnp.where(eye, ow_ref[...], 0.0), axis=1, keepdims=True)
+    own_out[0:quarter, :] = own
+    own_out[quarter : quarter + channels, :] = jnp.broadcast_to(column, (channels, channels))
+    n_slab, hslot = halo_ref.shape[0], halo_ref.shape[2]
+    onehot = owner_onehot(halo_ref[:, 0, :].astype(F32), n_slab * hslot, turned_out.shape[0], hslot)
+    turned_out[...] = onehot.astype(F32).T.astype(BF)
 
 
 def radial(k, slots, w_ref, b_ref, lanes):
@@ -251,7 +264,7 @@
     me_ref, *refs,
 ):
     sums = refs[:parts]
-    pw_ref, ow_ref, cot_ref, y_ref, hot_ref, r_ref = refs[parts : parts + 6]
+    pw_ref, own_ref, cot_ref, y_ref, hot_ref, r_ref = refs[parts : parts + 6]
     grads_ref, density_ref, s_all, ds, z, acc, dens = refs[parts + 6 :]
     slots = y_ref.shape[0]
     me = me_ref[0]
@@ -259,20 +272,16 @@
     for j in range(parts):
         at = pl.multiple_of((me ^ j) * quarter, quarter)
         s_all[pl.ds(at, quarter), :] = sums[j][...].astype(F32)
-    pw = pw_ref[...]
-    p_high, p_low = split(pw)
     given = s_all[...].astype(BF)
-    pre = dot_tn(p_high, given) + dot_tn(p_low, given)
-    eye = iota((channels, channels), 0) == iota((channels, channels), 1)
-    ow = jnp.sum(jnp.where(eye, ow_ref[...], 0.0), axis=1, keepdims=True)
+    pre = dot_nn(pw_ref[:, 0:channels], given) + dot_nn(pw_ref[:, channels : 2 * channels], given)
+    ow = own_ref[quarter : quarter + channels, 0:1]
     sigma = 1.0 / (1.0 + jnp.exp(-pre))
     dens[...] = jnp.sum(pre * sigma * ow, axis=0, keepdims=True)
     here = pl.multiple_of(me * probes, 128)
     density_ref[...] = dens[:, pl.ds(here, probes)]
     dpre = cot_ref[0:1, :] * ow * sigma * (1.0 + pre * (1.0 - sigma))
     d_high, d_low = split(dpre)
-    own = pl.multiple_of(me * quarter, quarter)
-    o_high, o_low = split(pw_ref[pl.ds(own, quarter), :])
+    o_high, o_low = split(own_ref[0:quarter, :])
     ds[...] = dot_nn(o_high, d_high) + dot_nn(o_high, d_low) + dot_nn(o_low, d_high)
     acc[...] = jnp.zeros_like(acc)
 
@@ -348,7 +357,7 @@
             pltpu.VMEM(offsets.shape, F32),
             pltpu.VMEM(probe_atoms.shape, jnp.int32),
             pltpu.VMEM((1, probes), F32),
-            pltpu.SemaphoreType.DMA((4 + groups,)),
+            pltpu.SemaphoreType.DMA((5,)),
         ],
         compiler_params=wide,
         name="pack",
@@ -356,23 +365,34 @@
     geo_blocks = spread_over(geometry, n_dom)
     halo = lax.all_to_all(send, ("slab", "dom"), split_axis=0, concat_axis=0, tiled=True)
 
-    y_all, cot, listed, basis, weights = pl.pallas_call(
-        functools.partial(basis_kernel, n_dom, channels, slots, probes),
-        in_specs=[smem] + [vmem] * (n_dom + 1),
-        out_specs=[vmem] * 5,
-        scratch_shapes=[
-            pltpu.VMEM((5 * slots, slab_probes), F32),
-        ],
+    weights, mixing, readout, turned = pl.pallas_call(
+        functools.partial(prepare_kernel, n_dom, channels, slots),
+        in_specs=[smem] + [vmem] * 4,
+        out_specs=[vmem] * 4,
+        out_shape=[
+            jax.ShapeDtypeStruct((5 * quarter, 3 * orders * slots), F32),
+            jax.ShapeDtypeStruct((channels, 2 * channels), BF),
+            jax.ShapeDtypeStruct((quarter + channels, channels), F32),
+            jax.ShapeDtypeStruct((atoms, n_slab * hslot), BF),
+        ],
+        compiler_params=narrow,
+        name="prepare",
+    )(me, radial_weights, probe_weight, out_weight.reshape(1, channels), halo_lists)
+
+    y_all, cot, listed, basis = pl.pallas_call(
+        functools.partial(basis_kernel, n_dom, orders, slots, probes),
+        in_specs=[smem] + [vmem] * n_dom,
+        out_specs=[vmem] * 4,
+        scratch_shapes=[pltpu.VMEM((5 * slots, slab_probes), F32)],
         out_shape=[
             jax.ShapeDtypeStruct((slots, 32, slab_probes), F32),
             jax.ShapeDtypeStruct((slots, slab_probes), F32),
             jax.ShapeDtypeStruct((slots, slab_probes), jnp.int32),
             jax.ShapeDtypeStruct((3 * orders * slots, slab_probes), BF),
-            jax.ShapeDtypeStruct((5 * quarter, 3 * orders * slots), F32),
         ],
         compiler_params=narrow,
         name="basis",
-    )(me, *geo_blocks, radial_weights)
+    )(me, *geo_blocks)
 
     sums, hot, r_all = pl.pallas_call(
         functools.partial(forward_kernel, quarter),
@@ -411,13 +431,13 @@
         compiler_params=narrow,
         name="backward",
     )(
-        me, *sum_blocks, probe_weight, out_weight.reshape(1, channels), cot, y_all,
+        me, *sum_blocks, mixing, readout, cot, y_all,
         hot, r_all,
     )
 
     back = lax.all_to_all(grads, ("slab", "dom"), split_axis=0, concat_axis=0, tiled=True)
     atom_grads = pl.pallas_call(
-        functools.partial(unpack_kernel, n_dom),
+        functools.partial(unpack_kernel, n_dom, hslot),
         in_specs=[vmem, vmem],
         out_specs=any_space,
         scratch_shapes=[
@@ -427,7 +447,7 @@
         out_shape=jax.ShapeDtypeStruct((atoms, feature_len), F32),
         compiler_params=narrow,
         name="unpack",
-    )(back, halo_lists)
+    )(back, turned)
     return (density.reshape(probes), atom_grads)
 
 

time: 62.3 us -> 59.5 us (0.955)
  waiting for transfers between devices: 14.8 us -> 12.4 us
  Pallas kernels: 16.2 us -> 15.2 us
  local copies, waits for them, and re-layouts: 3 us -> 3.68 us
    all_to_all x1, waiting for transfers between devices: 4.96 us -> 3.73 us  [shards(): lax.all_to_all(send, ('slab', 'dom'), split_axis=0, concat_axis=0, tiled=...]
    ppermute x6, waiting for transfers between devices: 9.88 us -> 8.69 us  [spread_over(): blocks[j | bit] = lax.ppermute(blocks[j], 'dom', pairs)]
    pallas_call x1, Pallas kernels: 3.62 us -> 2.54 us  [shards(): pl.pallas_call(functools.partial(pack_kernel, n_dom), in_specs=[any_space...]
    unnamed x10, local copies, waits for them, and re-layouts: 3 us -> 3.68 us
    pallas_call x2 -> x3, Pallas kernels: 2.5 us -> 2.53 us  [the longest x1 1.49 us: shards(): pl.pallas_call(functools.partial(unpack_kernel, n_dom, hslot), in_specs=[...]
  transfers between devices with their start and end apart: 7 -> 7, of which waited for: 5 -> 4; matrix products, arithmetic and copies ran while one was open for 0% -> 0% of each run, Pallas kernels for 1% -> 2%
where the time goes in v3:
time: 59.5 us; the launch traced here: 59.1 us
  blocking collectives  17 us (29%)
  Pallas kernels  15.2 us (26%)
  waiting for transfers between devices  12.4 us (21%)
  starting transfers between devices  10.1 us (17%)
  local copies, waits for them, and re-layouts  3.68 us (6%)
  between operations  0.71 us (1%)
    all_to_all x1, blocking collectives, shards(): lax.all_to_all(grads, ('slab', 'dom'), split_axis=0, concat_axis=0, tiled...  17 us
    ppermute x6, waiting for transfers between devices, spread_over(): blocks[j | bit] = lax.ppermute(blocks[j], 'dom', pairs)  8.69 us
    all_to_all x1, starting transfers between devices, shards(): lax.all_to_all(send, ('slab', 'dom'), split_axis=0, concat_axis=0, tiled=...  7.3 us
    pallas_call x1, Pallas kernels, shards(): pl.pallas_call(functools.partial(forward_kernel, quarter), in_specs=[vmem...  5.43 us
    pallas_call x1, Pallas kernels, shards(): pl.pallas_call(functools.partial(backward_kernel, n_dom, quarter, probes)...  4.69 us
    all_to_all x1, waiting for transfers between devices, shards(): lax.all_to_all(send, ('slab', 'dom'), split_axis=0, concat_axis=0, tiled=...  3.73 us
    unnamed x10, local copies, waits for them, and re-layouts  3.68 us
    ppermute x6, starting transfers between devices, spread_over(): blocks[j | bit] = lax.ppermute(blocks[j], 'dom', pairs)  2.77 us
  transfers between devices with their start and end apart: 7, of which 4 were waited for; matrix products, arithmetic and copies ran while one was open for 0% of the time, Pallas kernels for 2%

profile of v3, /device:TPU:0, one launch (start us, length us, event | category | flops | bytes accessed | tf_op | source)
XLA Modules:
  0.0 59.1 jit_solution(9453033455345291606)
XLA Ops:
  0.6 2.5 %pack.1 = (bf16[256,896]{1,0:T(8,128)(2,1)}, f32[40,256]{1,0:T(8,128)}) custom-call(bf16[128,3200]{1,0:T(8,128)(2,1)} %h_hbm.1, s32[8,1,8]{2,1,0:T(1,128)} %halo_ref.1, f32[3,8,256]{2,1,0:T(8,128)} %off_hbm.1, s32[8,256]{1,0:T(8,128)} %atoms_hbm.1, f32[1,256]{1,0:T(1,128)} %bitcast.13), custom_call_target="tpu_custom_call" | custom-call | tf_op jit(solution)/shard_map/pack/pallas_call | solution.py:346
  3.2 7.3 %all-to-all-start = ((bf16[32,8,896]{2,1,0:T(8,128)(2,1)}), bf16[32,8,896]{2,1,0:T(8,128)(2,1)S(1)}, u32[]{:S(2)}, u32[]{:S(2)}) async-start(bf16[32,8,896]{2,1,0:T(8,128)(2,1)} %bitcast.12), calls=%async_computation | async-start | bytes 917504 | tf_op jit(solution)/shard_map/all_to_all | solution.py:366
  10.5 1.8 %collective-permute-start.1 = (f32[40,256]{1,0:T(8,128)}, f32[40,256]{1,0:T(8,128)S(1)}, u32[]{:S(2)}, u32[]{:S(2)}) collective-permute-start(f32[40,256]{1,0:T(8,128)} %get-tuple-element.18.refs_0_), channel_id=1, source_target_pairs={{0,2},{1,3},{2,0},{3,1},{4,6},{5,7},{6,4},{7,5},{8,10},{9,11},{10,... | collective-permute-start | bytes 122888 | tf_op jit(solution)/shard_map/ppermute | solution.py:312
  12.3 0.0 collective-permute-start
  12.3 4.0 %collective-permute-done.1.refs_2_ = f32[40,256]{1,0:T(8,128)S(1)} collective-permute-done((f32[40,256]{1,0:T(8,128)}, f32[40,256]{1,0:T(8,128)S(1)}, u32[]{:S(2)}, u32[]{:S(2)}) %collective-permute-start.1) | collective-permute-done | bytes 40992 | tf_op jit(solution)/shard_map/ppermute | solution.py:312
  16.3 0.0 collective-permute-start.2
  16.4 0.0 copy-start
  16.4 0.8 %copy-done = f32[128,128]{1,0:T(8,128)S(1)} copy-done((f32[128,128]{1,0:T(8,128)S(1)}, f32[128,128]{1,0:T(8,128)}, u32[]{:S(2)}) %copy-start) | copy-done | bytes 65560
  17.2 0.0 copy-start.2
  17.2 0.7 %copy-done.2 = f32[8,640]{1,0:T(8,128)S(1)} copy-done((f32[8,640]{1,0:T(8,128)S(1)}, f32[8,640]{1,0:T(8,128)}, u32[]{:S(2)}) %copy-start.2) | copy-done | bytes 20504
  17.9 0.0 copy-start.3
  17.9 0.7 %copy-done.3 = s32[8,1,8]{2,1,0:T(1,128)S(1)} copy-done((s32[8,1,8]{2,1,0:T(1,128)S(1)}, s32[8,1,8]{2,1,0:T(1,128)}, u32[]{:S(2)}) %copy-start.3) | copy-done | bytes 280
  18.6 0.0 copy-start.4
  18.6 0.7 %copy-done.4 = f32[128]{0:T(128)S(1)} copy-done((f32[128]{0:T(128)S(1)}, f32[128]{0:T(128)}, u32[]{:S(2)}) %copy-start.4) | copy-done | bytes 536
  19.3 0.5 prepare.1
  19.7 0.0 collective-permute-done.refs_1_
  19.7 0.0 collective-permute-done.2.refs_3_
  19.8 0.0 copy-start.1
  19.8 0.8 %copy-done.1 = f32[40,256]{1,0:T(8,128)S(1)} copy-done((f32[40,256]{1,0:T(8,128)S(1)}, f32[40,256]{1,0:T(8,128)}, u32[]{:S(2)}) %copy-start.1) | copy-done | bytes 40984
  20.5 0.6 basis.1
  21.1 3.7 %all-to-all-done = bf16[32,8,896]{2,1,0:T(8,128)(2,1)S(1)} async-done(((bf16[32,8,896]{2,1,0:T(8,128)(2,1)}), bf16[32,8,896]{2,1,0:T(8,128)(2,1)S(1)}, u32[]{:S(2)}, u32[]{:S(2)}) %all-to-all-start) | async-done | bytes 458784 | tf_op jit(solution)/shard_map/all_to_all | solution.py:366
  24.8 5.4 %forward.1 = (bf16[32,1024]{1,0:T(8,128)(2,1)S(1)}, bf16[8,256,1024]{2,1,0:T(8,128)(2,1)S(1)}, f32[8,160,1024]{2,1,0:T(8,128)S(1)}) custom-call(bf16[256,896]{1,0:T(8,128)(2,1)S(1)} %bitcast.8, f32[8,32,1024]{2,1,0:T(8,128)S(1)} %get-tuple-element.19.y_ref.refs_7_, s32[8,1024]{1,0:T(8,128)S(1)} %get-tuple-element.20.atoms_ref, ...), custom_call_target="tpu_custom_call" | custom-call | tf_op jit(solution)/shard_map/forward/pallas_call | solution.py:397
  30.3 0.8 %collective-permute-start.4 = (bf16[32,1024]{1,0:T(8,128)(2,1)S(1)}, bf16[32,1024]{1,0:T(8,128)(2,1)S(1)}, u32[]{:S(2)}, u32[]{:S(2)}) collective-permute-start(bf16[32,1024]{1,0:T(8,128)(2,1)S(1)} %get-tuple-element.23.refs_0_), channel_id=1, source_target_pairs={{0,2},{1,3},{2,0},{3,1},{4,6},{5,7},{6,4},{7,5},{8,10},{9,11},{10,... | collective-permute-start | bytes 196616 | tf_op jit(solution)/shard_map/ppermute | solution.py:312
  31.0 0.2 collective-permute-start.3
  31.2 3.4 %collective-permute-done.4.refs_2_ = bf16[32,1024]{1,0:T(8,128)(2,1)S(1)} collective-permute-done((bf16[32,1024]{1,0:T(8,128)(2,1)S(1)}, bf16[32,1024]{1,0:T(8,128)(2,1)S(1)}, u32[]{:S(2)}, u32[]{:S(2)}) %collective-permute-start.4) | collective-permute-done | bytes 65568 | tf_op jit(solution)/shard_map/ppermute | solution.py:312
  34.6 0.0 collective-permute-start.5
  34.6 0.0 collective-permute-done.3.refs_1_
  34.6 1.2 %collective-permute-done.5.refs_3_ = bf16[32,1024]{1,0:T(8,128)(2,1)S(1)} collective-permute-done((bf16[32,1024]{1,0:T(8,128)(2,1)S(1)}, bf16[32,1024]{1,0:T(8,128)(2,1)S(1)}, u32[]{:S(2)}, u32[]{:S(2)}) %collective-permute-start.5) | collective-permute-done | bytes 65568 | tf_op jit(solution)/shard_map/ppermute | solution.py:312
  35.9 4.7 %backward.1 = (bf16[256,896]{1,0:T(8,128)(2,1)S(1)}, f32[1,256]{1,0:T(1,128)}) custom-call(s32[1]{0:T(128)} %bitcast.me_ref, bf16[32,1024]{1,0:T(8,128)(2,1)S(1)} %get-tuple-element.23.refs_0_, bf16[32,1024]{1,0:T(8,128)(2,1)S(1)} %collective-permute-done.3.refs_1_, bf16[32,1024]{1,0:T(8,128)(2,1)S(1)} %collective-permute-done.4.refs_2_, ...), custom_call_target="tpu_custom_call" | custom-call | tf_op jit(solution)/shard_map/backward/pallas_call | solution.py:416
  40.6 17.0 %all_to_all.22 = bf16[32,8,896]{2,1,0:T(8,128)(2,1)S(1)} all-to-all(bf16[32,8,896]{2,1,0:T(8,128)(2,1)S(1)} %bitcast.10), channel_id=1, replica_groups=mesh['slab'=8,'dom'=4] {'slab','dom'}, dimensions={0} | all-to-all | bytes 917504 | tf_op jit(solution)/shard_map/all_to_all | solution.py:438
  57.6 1.5 %unpack.1 = f32[128,3200]{1,0:T(8,128)} custom-call(bf16[256,896]{1,0:T(8,128)(2,1)S(1)} %bitcast.9, bf16[128,64]{1,0:T(8,128)(2,1)S(1)} %get-tuple-element.31.turned_ref), custom_call_target="tpu_custom_call" | custom-call | tf_op jit(solution)/shard_map/unpack/pallas_call | solution.py:439
Async XLA Ops:
  3.2 21.7 %all-to-all-start = ((bf16[32,8,896]{2,1,0:T(8,128)(2,1)}), bf16[32,8,896]{2,1,0:T(8,128)(2,1)S(1)}, u32[]{:S(2)}, u32[]{:S(2)}) async-start(bf16[32,8,896]{2,1,0:T(8,128)(2,1)} %bitcast.12), calls=%async_computation | async-start | bytes 917504 | tf_op jit(solution)/shard_map/all_to_all | solution.py:366
  10.5 5.9 %collective-permute-start.1 = (f32[40,256]{1,0:T(8,128)}, f32[40,256]{1,0:T(8,128)S(1)}, u32[]{:S(2)}, u32[]{:S(2)}) collective-permute-start(f32[40,256]{1,0:T(8,128)} %get-tuple-element.18.refs_0_), channel_id=1, source_target_pairs={{0,2},{1,3},{2,0},{3,1},{4,6},{5,7},{6,4},{7,5},{8,10},{9,11},{10,... | collective-permute-start | bytes 122888 | tf_op jit(solution)/shard_map/ppermute | solution.py:312
  12.3 7.4 %collective-permute-start = (f32[40,256]{1,0:T(8,128)}, f32[40,256]{1,0:T(8,128)S(1)}, u32[]{:S(2)}, u32[]{:S(2)}) collective-permute-start(f32[40,256]{1,0:T(8,128)} %get-tuple-element.18.refs_0_), channel_id=1, source_target_pairs={{0,1},{1,0},{2,3},{3,2},{4,5},{5,4},{6,7},{7,6},{8,9},{9,8},{10,11... | collective-permute-start | bytes 122888 | tf_op jit(solution)/shard_map/ppermute | solution.py:312
  16.3 3.4 %collective-permute-start.2 = (f32[40,256]{1,0:T(8,128)S(1)}, f32[40,256]{1,0:T(8,128)S(1)}, u32[]{:S(2)}, u32[]{:S(2)}) collective-permute-start(f32[40,256]{1,0:T(8,128)S(1)} %collective-permute-done.1.refs_2_), channel_id=1, source_target_pairs={{0,1},{1,0},{2,3},{3,2},{4,5},{5,4},{6,7},{7,6},{8,9},{9,8},{10,11... | collective-permute-start | bytes 122888 | tf_op jit(solution)/shard_map/ppermute | solution.py:312
  16.4 0.8 %copy-start = (f32[128,128]{1,0:T(8,128)S(1)}, f32[128,128]{1,0:T(8,128)}, u32[]{:S(2)}) copy-start(f32[128,128]{1,0:T(8,128)} %pw_ref.1) | copy-start | bytes 196612
  17.2 0.7 %copy-start.2 = (f32[8,640]{1,0:T(8,128)S(1)}, f32[8,640]{1,0:T(8,128)}, u32[]{:S(2)}) copy-start(f32[8,640]{1,0:T(8,128)} %weight_ref.1) | copy-start | bytes 61444
  17.9 0.7 %copy-start.3 = (s32[8,1,8]{2,1,0:T(1,128)S(1)}, s32[8,1,8]{2,1,0:T(1,128)}, u32[]{:S(2)}) copy-start(s32[8,1,8]{2,1,0:T(1,128)} %halo_ref.1) | copy-start | bytes 772
  18.6 0.7 %copy-start.4 = (f32[128]{0:T(128)S(1)}, f32[128]{0:T(128)}, u32[]{:S(2)}) copy-start(f32[128]{0:T(128)} %param.14) | copy-start | bytes 1540
  19.8 0.8 %copy-start.1 = (f32[40,256]{1,0:T(8,128)S(1)}, f32[40,256]{1,0:T(8,128)}, u32[]{:S(2)}) copy-start(f32[40,256]{1,0:T(8,128)} %get-tuple-element.18.refs_0_) | copy-start | bytes 122884
  30.3 4.3 %collective-permute-start.4 = (bf16[32,1024]{1,0:T(8,128)(2,1)S(1)}, bf16[32,1024]{1,0:T(8,128)(2,1)S(1)}, u32[]{:S(2)}, u32[]{:S(2)}) collective-permute-start(bf16[32,1024]{1,0:T(8,128)(2,1)S(1)} %get-tuple-element.23.refs_0_), channel_id=1, source_target_pairs={{0,2},{1,3},{2,0},{3,1},{4,6},{5,7},{6,4},{7,5},{8,10},{9,11},{10,... | collective-permute-start | bytes 196616 | tf_op jit(solution)/shard_map/ppermute | solution.py:312
  31.0 3.6 %collective-permute-start.3 = (bf16[32,1024]{1,0:T(8,128)(2,1)S(1)}, bf16[32,1024]{1,0:T(8,128)(2,1)S(1)}, u32[]{:S(2)}, u32[]{:S(2)}) collective-permute-start(bf16[32,1024]{1,0:T(8,128)(2,1)S(1)} %get-tuple-element.23.refs_0_), channel_id=1, source_target_pairs={{0,1},{1,0},{2,3},{3,2},{4,5},{5,4},{6,7},{7,6},{8,9},{9,8},{10,11... | collective-permute-start | bytes 196616 | tf_op jit(solution)/shard_map/ppermute | solution.py:312
  34.6 1.3 %collective-permute-start.5 = (bf16[32,1024]{1,0:T(8,128)(2,1)S(1)}, bf16[32,1024]{1,0:T(8,128)(2,1)S(1)}, u32[]{:S(2)}, u32[]{:S(2)}) collective-permute-start(bf16[32,1024]{1,0:T(8,128)(2,1)S(1)} %collective-permute-done.4.refs_2_), channel_id=1, source_target_pairs={{0,1},{1,0},{2,3},{3,2},{4,5},{5,4},{6,7},{7,6},{8,9},{9,8},{10,11... | collective-permute-start | bytes 196616 | tf_op jit(solution)/shard_map/ppermute | solution.py:312

commit v4 on v3

--- a/solution.py
+++ b/solution.py
@@ -235,27 +235,21 @@
     slots, table = atoms_ref.shape[0], h_ref.shape[0]
     turned[...] = h_ref[...].astype(F32).T.astype(BF)
     total[...] = jnp.zeros_like(total)
-    width = total.shape[1]
-    step = 256
-
     for k in range(slots):
-        for at in range(0, width, step):
-            lanes = slice(at, at + step)
-            hot = onehot_of(k, atoms_ref, table, lanes)
-            rad = radial(k, slots, w_ref, b_ref, lanes)
-            hot_ref[k, :, lanes] = hot
-            r_ref[k, :, lanes] = rad
-            got = dot_nn(turned[0 : COMPONENTS * quarter, :], hot)
-            acc = total[:, lanes]
-            for degree in range(5):
-                first, last = degree * degree, (degree + 1) ** 2
-                inner = got[first * quarter : (first + 1) * quarter] * y_ref[k, first : first + 1, lanes]
-                for m in range(first + 1, last):
-                    inner = inner + (
-                        got[m * quarter : (m + 1) * quarter] * y_ref[k, m : m + 1, lanes]
-                    )
-                acc = acc + inner * rad[degree * quarter : (degree + 1) * quarter]
-            total[:, lanes] = acc
+        hot = onehot_of(k, atoms_ref, table, slice(None))
+        rad = radial(k, slots, w_ref, b_ref, slice(None))
+        hot_ref[k] = hot
+        r_ref[k] = rad
+        got = dot_nn(turned[0 : COMPONENTS * quarter, :], hot)
+        acc = total[...]
+        for degree in range(5):
+            first, last = degree * degree, (degree + 1) ** 2
+            inner = got[first * quarter : (first + 1) * quarter] * y_ref[k, first : first + 1, :]
+            for m in range(first + 1, last):
+                inner = inner + got[m * quarter : (m + 1) * quarter] * y_ref[k, m : m + 1, :]
+            acc = acc + inner * rad[degree * quarter : (degree + 1) * quarter]
+        total[...] = acc
+
     s_ref[...] = total[...].astype(BF)
 
 

time: 59.5 us -> 59.1 us (level)
  no operation moved by 1% of the time
where the time goes in v4:
time: 59.1 us; the launch traced here: 58.7 us
  blocking collectives  17 us (29%)
  Pallas kernels  14.8 us (25%)
  waiting for transfers between devices  12.4 us (21%)
  starting transfers between devices  10.1 us (17%)
  local copies, waits for them, and re-layouts  3.68 us (6%)
  between operations  0.71 us (1%)
    all_to_all x1, blocking collectives, shards(): lax.all_to_all(grads, ('slab', 'dom'), split_axis=0, concat_axis=0, tiled...  17 us
    ppermute x6, waiting for transfers between devices, spread_over(): blocks[j | bit] = lax.ppermute(blocks[j], 'dom', pairs)  8.67 us
    all_to_all x1, starting transfers between devices, shards(): lax.all_to_all(send, ('slab', 'dom'), split_axis=0, concat_axis=0, tiled=...  7.3 us
    pallas_call x1, Pallas kernels, shards(): pl.pallas_call(functools.partial(forward_kernel, quarter), in_specs=[vmem...  5 us
    pallas_call x1, Pallas kernels, shards(): pl.pallas_call(functools.partial(backward_kernel, n_dom, quarter, probes)...  4.68 us
    all_to_all x1, waiting for transfers between devices, shards(): lax.all_to_all(send, ('slab', 'dom'), split_axis=0, concat_axis=0, tiled=...  3.73 us
    unnamed x10, local copies, waits for them, and re-layouts  3.68 us
    ppermute x6, starting transfers between devices, spread_over(): blocks[j | bit] = lax.ppermute(blocks[j], 'dom', pairs)  2.78 us
  transfers between devices with their start and end apart: 7, of which 4 were waited for; matrix products, arithmetic and copies ran while one was open for 0% of the time, Pallas kernels for 2%

profile of v4, /device:TPU:0, one launch (start us, length us, event | category | flops | bytes accessed | tf_op | source)
XLA Modules:
  0.0 58.7 jit_solution(15571132064428722984)
XLA Ops:
  0.6 2.5 %pack.1 = (bf16[256,896]{1,0:T(8,128)(2,1)}, f32[40,256]{1,0:T(8,128)}) custom-call(bf16[128,3200]{1,0:T(8,128)(2,1)} %h_hbm.1, s32[8,1,8]{2,1,0:T(1,128)} %halo_ref.1, f32[3,8,256]{2,1,0:T(8,128)} %off_hbm.1, s32[8,256]{1,0:T(8,128)} %atoms_hbm.1, f32[1,256]{1,0:T(1,128)} %bitcast.13), custom_call_target="tpu_custom_call" | custom-call | tf_op jit(solution)/shard_map/pack/pallas_call | solution.py:340
  3.2 7.3 %all-to-all-start = ((bf16[32,8,896]{2,1,0:T(8,128)(2,1)}), bf16[32,8,896]{2,1,0:T(8,128)(2,1)S(1)}, u32[]{:S(2)}, u32[]{:S(2)}) async-start(bf16[32,8,896]{2,1,0:T(8,128)(2,1)} %bitcast.12), calls=%async_computation | async-start | bytes 917504 | tf_op jit(solution)/shard_map/all_to_all | solution.py:360
  10.5 1.8 %collective-permute-start.1 = (f32[40,256]{1,0:T(8,128)}, f32[40,256]{1,0:T(8,128)S(1)}, u32[]{:S(2)}, u32[]{:S(2)}) collective-permute-start(f32[40,256]{1,0:T(8,128)} %get-tuple-element.18.refs_0_), channel_id=1, source_target_pairs={{0,2},{1,3},{2,0},{3,1},{4,6},{5,7},{6,4},{7,5},{8,10},{9,11},{10,... | collective-permute-start | bytes 122888 | tf_op jit(solution)/shard_map/ppermute | solution.py:306
  12.3 0.0 collective-permute-start
  12.3 4.0 %collective-permute-done.1.refs_2_ = f32[40,256]{1,0:T(8,128)S(1)} collective-permute-done((f32[40,256]{1,0:T(8,128)}, f32[40,256]{1,0:T(8,128)S(1)}, u32[]{:S(2)}, u32[]{:S(2)}) %collective-permute-start.1) | collective-permute-done | bytes 40992 | tf_op jit(solution)/shard_map/ppermute | solution.py:306
  16.3 0.0 collective-permute-start.2
  16.4 0.0 copy-start
  16.4 0.8 %copy-done = f32[128,128]{1,0:T(8,128)S(1)} copy-done((f32[128,128]{1,0:T(8,128)S(1)}, f32[128,128]{1,0:T(8,128)}, u32[]{:S(2)}) %copy-start) | copy-done | bytes 65560
  17.2 0.0 copy-start.2
  17.2 0.7 %copy-done.2 = f32[8,640]{1,0:T(8,128)S(1)} copy-done((f32[8,640]{1,0:T(8,128)S(1)}, f32[8,640]{1,0:T(8,128)}, u32[]{:S(2)}) %copy-start.2) | copy-done | bytes 20504
  17.9 0.0 copy-start.3
  17.9 0.7 %copy-done.3 = s32[8,1,8]{2,1,0:T(1,128)S(1)} copy-done((s32[8,1,8]{2,1,0:T(1,128)S(1)}, s32[8,1,8]{2,1,0:T(1,128)}, u32[]{:S(2)}) %copy-start.3) | copy-done | bytes 280
  18.6 0.0 copy-start.4
  18.6 0.7 %copy-done.4 = f32[128]{0:T(128)S(1)} copy-done((f32[128]{0:T(128)S(1)}, f32[128]{0:T(128)}, u32[]{:S(2)}) %copy-start.4) | copy-done | bytes 536
  19.3 0.5 prepare.1
  19.7 0.0 collective-permute-done.refs_1_
  19.7 0.0 collective-permute-done.2.refs_3_
  19.8 0.0 copy-start.1
  19.8 0.8 %copy-done.1 = f32[40,256]{1,0:T(8,128)S(1)} copy-done((f32[40,256]{1,0:T(8,128)S(1)}, f32[40,256]{1,0:T(8,128)}, u32[]{:S(2)}) %copy-start.1) | copy-done | bytes 40984
  20.5 0.6 basis.1
  21.1 3.7 %all-to-all-done = bf16[32,8,896]{2,1,0:T(8,128)(2,1)S(1)} async-done(((bf16[32,8,896]{2,1,0:T(8,128)(2,1)}), bf16[32,8,896]{2,1,0:T(8,128)(2,1)S(1)}, u32[]{:S(2)}, u32[]{:S(2)}) %all-to-all-start) | async-done | bytes 458784 | tf_op jit(solution)/shard_map/all_to_all | solution.py:360
  24.8 5.0 %forward.1 = (bf16[32,1024]{1,0:T(8,128)(2,1)S(1)}, bf16[8,256,1024]{2,1,0:T(8,128)(2,1)S(1)}, f32[8,160,1024]{2,1,0:T(8,128)S(1)}) custom-call(bf16[256,896]{1,0:T(8,128)(2,1)S(1)} %bitcast.8, f32[8,32,1024]{2,1,0:T(8,128)S(1)} %get-tuple-element.19.y_ref.refs_7_, s32[8,1024]{1,0:T(8,128)S(1)} %get-tuple-element.20.atoms_ref, ...), custom_call_target="tpu_custom_call" | custom-call | tf_op jit(solution)/shard_map/forward/pallas_call | solution.py:391
  29.9 0.8 %collective-permute-start.4 = (bf16[32,1024]{1,0:T(8,128)(2,1)S(1)}, bf16[32,1024]{1,0:T(8,128)(2,1)S(1)}, u32[]{:S(2)}, u32[]{:S(2)}) collective-permute-start(bf16[32,1024]{1,0:T(8,128)(2,1)S(1)} %get-tuple-element.23.refs_0_), channel_id=1, source_target_pairs={{0,2},{1,3},{2,0},{3,1},{4,6},{5,7},{6,4},{7,5},{8,10},{9,11},{10,... | collective-permute-start | bytes 196616 | tf_op jit(solution)/shard_map/ppermute | solution.py:306
  30.6 0.2 collective-permute-start.3
  30.8 3.4 %collective-permute-done.4.refs_2_ = bf16[32,1024]{1,0:T(8,128)(2,1)S(1)} collective-permute-done((bf16[32,1024]{1,0:T(8,128)(2,1)S(1)}, bf16[32,1024]{1,0:T(8,128)(2,1)S(1)}, u32[]{:S(2)}, u32[]{:S(2)}) %collective-permute-start.4) | collective-permute-done | bytes 65568 | tf_op jit(solution)/shard_map/ppermute | solution.py:306
  34.2 0.0 collective-permute-start.5
  34.2 0.0 collective-permute-done.3.refs_1_
  34.2 1.2 %collective-permute-done.5.refs_3_ = bf16[32,1024]{1,0:T(8,128)(2,1)S(1)} collective-permute-done((bf16[32,1024]{1,0:T(8,128)(2,1)S(1)}, bf16[32,1024]{1,0:T(8,128)(2,1)S(1)}, u32[]{:S(2)}, u32[]{:S(2)}) %collective-permute-start.5) | collective-permute-done | bytes 65568 | tf_op jit(solution)/shard_map/ppermute | solution.py:306
  35.4 4.7 %backward.1 = (bf16[256,896]{1,0:T(8,128)(2,1)S(1)}, f32[1,256]{1,0:T(1,128)}) custom-call(s32[1]{0:T(128)} %bitcast.me_ref, bf16[32,1024]{1,0:T(8,128)(2,1)S(1)} %get-tuple-element.23.refs_0_, bf16[32,1024]{1,0:T(8,128)(2,1)S(1)} %collective-permute-done.3.refs_1_, bf16[32,1024]{1,0:T(8,128)(2,1)S(1)} %collective-permute-done.4.refs_2_, ...), custom_call_target="tpu_custom_call" | custom-call | tf_op jit(solution)/shard_map/backward/pallas_call | solution.py:410
  40.1 17.0 %all_to_all.22 = bf16[32,8,896]{2,1,0:T(8,128)(2,1)S(1)} all-to-all(bf16[32,8,896]{2,1,0:T(8,128)(2,1)S(1)} %bitcast.10), channel_id=1, replica_groups=mesh['slab'=8,'dom'=4] {'slab','dom'}, dimensions={0} | all-to-all | bytes 917504 | tf_op jit(solution)/shard_map/all_to_all | solution.py:432
  57.2 1.5 %unpack.1 = f32[128,3200]{1,0:T(8,128)} custom-call(bf16[256,896]{1,0:T(8,128)(2,1)S(1)} %bitcast.9, bf16[128,64]{1,0:T(8,128)(2,1)S(1)} %get-tuple-element.31.turned_ref), custom_call_target="tpu_custom_call" | custom-call | tf_op jit(solution)/shard_map/unpack/pallas_call | solution.py:433
Async XLA Ops:
  3.2 21.7 %all-to-all-start = ((bf16[32,8,896]{2,1,0:T(8,128)(2,1)}), bf16[32,8,896]{2,1,0:T(8,128)(2,1)S(1)}, u32[]{:S(2)}, u32[]{:S(2)}) async-start(bf16[32,8,896]{2,1,0:T(8,128)(2,1)} %bitcast.12), calls=%async_computation | async-start | bytes 917504 | tf_op jit(solution)/shard_map/all_to_all | solution.py:360
  10.5 5.9 %collective-permute-start.1 = (f32[40,256]{1,0:T(8,128)}, f32[40,256]{1,0:T(8,128)S(1)}, u32[]{:S(2)}, u32[]{:S(2)}) collective-permute-start(f32[40,256]{1,0:T(8,128)} %get-tuple-element.18.refs_0_), channel_id=1, source_target_pairs={{0,2},{1,3},{2,0},{3,1},{4,6},{5,7},{6,4},{7,5},{8,10},{9,11},{10,... | collective-permute-start | bytes 122888 | tf_op jit(solution)/shard_map/ppermute | solution.py:306
  12.3 7.4 %collective-permute-start = (f32[40,256]{1,0:T(8,128)}, f32[40,256]{1,0:T(8,128)S(1)}, u32[]{:S(2)}, u32[]{:S(2)}) collective-permute-start(f32[40,256]{1,0:T(8,128)} %get-tuple-element.18.refs_0_), channel_id=1, source_target_pairs={{0,1},{1,0},{2,3},{3,2},{4,5},{5,4},{6,7},{7,6},{8,9},{9,8},{10,11... | collective-permute-start | bytes 122888 | tf_op jit(solution)/shard_map/ppermute | solution.py:306
  16.3 3.4 %collective-permute-start.2 = (f32[40,256]{1,0:T(8,128)S(1)}, f32[40,256]{1,0:T(8,128)S(1)}, u32[]{:S(2)}, u32[]{:S(2)}) collective-permute-start(f32[40,256]{1,0:T(8,128)S(1)} %collective-permute-done.1.refs_2_), channel_id=1, source_target_pairs={{0,1},{1,0},{2,3},{3,2},{4,5},{5,4},{6,7},{7,6},{8,9},{9,8},{10,11... | collective-permute-start | bytes 122888 | tf_op jit(solution)/shard_map/ppermute | solution.py:306
  16.4 0.8 %copy-start = (f32[128,128]{1,0:T(8,128)S(1)}, f32[128,128]{1,0:T(8,128)}, u32[]{:S(2)}) copy-start(f32[128,128]{1,0:T(8,128)} %pw_ref.1) | copy-start | bytes 196612
  17.2 0.7 %copy-start.2 = (f32[8,640]{1,0:T(8,128)S(1)}, f32[8,640]{1,0:T(8,128)}, u32[]{:S(2)}) copy-start(f32[8,640]{1,0:T(8,128)} %weight_ref.1) | copy-start | bytes 61444
  17.9 0.7 %copy-start.3 = (s32[8,1,8]{2,1,0:T(1,128)S(1)}, s32[8,1,8]{2,1,0:T(1,128)}, u32[]{:S(2)}) copy-start(s32[8,1,8]{2,1,0:T(1,128)} %halo_ref.1) | copy-start | bytes 772
  18.6 0.7 %copy-start.4 = (f32[128]{0:T(128)S(1)}, f32[128]{0:T(128)}, u32[]{:S(2)}) copy-start(f32[128]{0:T(128)} %param.14) | copy-start | bytes 1540
  19.8 0.8 %copy-start.1 = (f32[40,256]{1,0:T(8,128)S(1)}, f32[40,256]{1,0:T(8,128)}, u32[]{:S(2)}) copy-start(f32[40,256]{1,0:T(8,128)} %get-tuple-element.18.refs_0_) | copy-start | bytes 122884
  29.9 4.3 %collective-permute-start.4 = (bf16[32,1024]{1,0:T(8,128)(2,1)S(1)}, bf16[32,1024]{1,0:T(8,128)(2,1)S(1)}, u32[]{:S(2)}, u32[]{:S(2)}) collective-permute-start(bf16[32,1024]{1,0:T(8,128)(2,1)S(1)} %get-tuple-element.23.refs_0_), channel_id=1, source_target_pairs={{0,2},{1,3},{2,0},{3,1},{4,6},{5,7},{6,4},{7,5},{8,10},{9,11},{10,... | collective-permute-start | bytes 196616 | tf_op jit(solution)/shard_map/ppermute | solution.py:306
  30.6 3.6 %collective-permute-start.3 = (bf16[32,1024]{1,0:T(8,128)(2,1)S(1)}, bf16[32,1024]{1,0:T(8,128)(2,1)S(1)}, u32[]{:S(2)}, u32[]{:S(2)}) collective-permute-start(bf16[32,1024]{1,0:T(8,128)(2,1)S(1)} %get-tuple-element.23.refs_0_), channel_id=1, source_target_pairs={{0,1},{1,0},{2,3},{3,2},{4,5},{5,4},{6,7},{7,6},{8,9},{9,8},{10,11... | collective-permute-start | bytes 196616 | tf_op jit(solution)/shard_map/ppermute | solution.py:306
  34.2 1.3 %collective-permute-start.5 = (bf16[32,1024]{1,0:T(8,128)(2,1)S(1)}, bf16[32,1024]{1,0:T(8,128)(2,1)S(1)}, u32[]{:S(2)}, u32[]{:S(2)}) collective-permute-start(bf16[32,1024]{1,0:T(8,128)(2,1)S(1)} %collective-permute-done.4.refs_2_), channel_id=1, source_target_pairs={{0,1},{1,0},{2,3},{3,2},{4,5},{5,4},{6,7},{7,6},{8,9},{9,8},{10,11... | collective-permute-start | bytes 196616 | tf_op jit(solution)/shard_map/ppermute | solution.py:306

commit v5 on v4

--- a/solution.py
+++ b/solution.py
@@ -134,15 +134,16 @@
         got = recv_ref[:, group * 128 : (group + 1) * 128].astype(F32)
         got = got.reshape(n_slab, parts, hslot, 128)
         pieces = [got[:, part].reshape(rows, 128) for part in range(parts)]
+        placed = []
         for i in range(members):
             total = jnp.zeros((rows, 128), F32)
             for part in range(parts):
                 shift = ((part - i) * quarter) % 128
                 source = pltpu.roll(pieces[part], shift, 1) if shift else pieces[part]
                 total = jnp.where(lane_part == part, source, total)
-            at = (group * parts + i) * 128
-            out_ref[:, at : at + 128] = dot_nn(turned, total.astype(BF))
+            placed.append(total.astype(BF))
         lanes = slice(group * parts * 128, (group * parts + members) * 128)
+        out_ref[:, lanes] = dot_nn(turned, jnp.concatenate(placed, axis=1))
         copy = pltpu.make_async_copy(out_ref.at[:, lanes], out_hbm.at[:, lanes], sems.at[group])
         copy.start()
         copies.append(copy)
@@ -230,17 +231,16 @@
 
 
 def forward_kernel(
-    quarter, h_ref, y_ref, atoms_ref, b_ref, w_ref, s_ref, hot_ref, r_ref, turned, total
+    quarter, h_ref, y_ref, atoms_ref, b_ref, w_ref, s_ref, hot_ref, r_ref, total
 ):
     slots, table = atoms_ref.shape[0], h_ref.shape[0]
-    turned[...] = h_ref[...].astype(F32).T.astype(BF)
     total[...] = jnp.zeros_like(total)
     for k in range(slots):
         hot = onehot_of(k, atoms_ref, table, slice(None))
         rad = radial(k, slots, w_ref, b_ref, slice(None))
         hot_ref[k] = hot
         r_ref[k] = rad
-        got = dot_nn(turned[0 : COMPONENTS * quarter, :], hot)
+        got = dot_tn(h_ref[:, 0 : COMPONENTS * quarter], hot)
         acc = total[...]
         for degree in range(5):
             first, last = degree * degree, (degree + 1) ** 2
@@ -398,7 +398,6 @@
             jax.ShapeDtypeStruct((slots, 5 * quarter, slab_probes), F32),
         ],
         scratch_shapes=[
-            pltpu.VMEM((packed * n_dom // 128 * quarter, table), BF),
             pltpu.VMEM((quarter, slab_probes), F32),
         ],
         compiler_params=narrow,

time: 59.1 us -> 59.1 us (level)
  no operation moved by 1% of the time
where the time goes in v5:
time: 59.1 us; the launch traced here: 58.6 us
  blocking collectives  17 us (29%)
  Pallas kernels  14.7 us (25%)
  waiting for transfers between devices  12.4 us (21%)
  starting transfers between devices  10.1 us (17%)
  local copies, waits for them, and re-layouts  3.68 us (6%)
  between operations  0.71 us (1%)
    all_to_all x1, blocking collectives, shards(): lax.all_to_all(grads, ('slab', 'dom'), split_axis=0, concat_axis=0, tiled...  17 us
    ppermute x6, waiting for transfers between devices, spread_over(): blocks[j | bit] = lax.ppermute(blocks[j], 'dom', pairs)  8.69 us
    all_to_all x1, starting transfers between devices, shards(): lax.all_to_all(send, ('slab', 'dom'), split_axis=0, concat_axis=0, tiled=...  7.3 us
    pallas_call x1, Pallas kernels, shards(): pl.pallas_call(functools.partial(forward_kernel, quarter), in_specs=[vmem...  4.99 us
    pallas_call x1, Pallas kernels, shards(): pl.pallas_call(functools.partial(backward_kernel, n_dom, quarter, probes)...  4.68 us
    all_to_all x1, waiting for transfers between devices, shards(): lax.all_to_all(send, ('slab', 'dom'), split_axis=0, concat_axis=0, tiled=...  3.73 us
    unnamed x10, local copies, waits for them, and re-layouts  3.68 us
    ppermute x6, starting transfers between devices, spread_over(): blocks[j | bit] = lax.ppermute(blocks[j], 'dom', pairs)  2.77 us
  transfers between devices with their start and end apart: 7, of which 4 were waited for; matrix products, arithmetic and copies ran while one was open for 0% of the time, Pallas kernels for 2%

profile of v5, /device:TPU:0, one launch (start us, length us, event | category | flops | bytes accessed | tf_op | source)
XLA Modules:
  0.0 58.6 jit_solution(3016430966430924051)
XLA Ops:
  0.6 2.5 %pack.1 = (bf16[256,896]{1,0:T(8,128)(2,1)}, f32[40,256]{1,0:T(8,128)}) custom-call(bf16[128,3200]{1,0:T(8,128)(2,1)} %h_hbm.1, s32[8,1,8]{2,1,0:T(1,128)} %halo_ref.1, f32[3,8,256]{2,1,0:T(8,128)} %off_hbm.1, s32[8,256]{1,0:T(8,128)} %atoms_hbm.1, f32[1,256]{1,0:T(1,128)} %bitcast.13), custom_call_target="tpu_custom_call" | custom-call | tf_op jit(solution)/shard_map/pack/pallas_call | solution.py:340
  3.2 7.3 %all-to-all-start = ((bf16[32,8,896]{2,1,0:T(8,128)(2,1)}), bf16[32,8,896]{2,1,0:T(8,128)(2,1)S(1)}, u32[]{:S(2)}, u32[]{:S(2)}) async-start(bf16[32,8,896]{2,1,0:T(8,128)(2,1)} %bitcast.12), calls=%async_computation | async-start | bytes 917504 | tf_op jit(solution)/shard_map/all_to_all | solution.py:360
  10.5 1.8 %collective-permute-start.1 = (f32[40,256]{1,0:T(8,128)}, f32[40,256]{1,0:T(8,128)S(1)}, u32[]{:S(2)}, u32[]{:S(2)}) collective-permute-start(f32[40,256]{1,0:T(8,128)} %get-tuple-element.18.refs_0_), channel_id=1, source_target_pairs={{0,2},{1,3},{2,0},{3,1},{4,6},{5,7},{6,4},{7,5},{8,10},{9,11},{10,... | collective-permute-start | bytes 122888 | tf_op jit(solution)/shard_map/ppermute | solution.py:306
  12.3 0.0 collective-permute-start
  12.3 4.0 %collective-permute-done.1.refs_2_ = f32[40,256]{1,0:T(8,128)S(1)} collective-permute-done((f32[40,256]{1,0:T(8,128)}, f32[40,256]{1,0:T(8,128)S(1)}, u32[]{:S(2)}, u32[]{:S(2)}) %collective-permute-start.1) | collective-permute-done | bytes 40992 | tf_op jit(solution)/shard_map/ppermute | solution.py:306
  16.3 0.0 collective-permute-start.2
  16.4 0.0 copy-start
  16.4 0.8 %copy-done = f32[128,128]{1,0:T(8,128)S(1)} copy-done((f32[128,128]{1,0:T(8,128)S(1)}, f32[128,128]{1,0:T(8,128)}, u32[]{:S(2)}) %copy-start) | copy-done | bytes 65560
  17.2 0.0 copy-start.2
  17.2 0.7 %copy-done.2 = f32[8,640]{1,0:T(8,128)S(1)} copy-done((f32[8,640]{1,0:T(8,128)S(1)}, f32[8,640]{1,0:T(8,128)}, u32[]{:S(2)}) %copy-start.2) | copy-done | bytes 20504
  17.9 0.0 copy-start.3
  17.9 0.7 %copy-done.3 = s32[8,1,8]{2,1,0:T(1,128)S(1)} copy-done((s32[8,1,8]{2,1,0:T(1,128)S(1)}, s32[8,1,8]{2,1,0:T(1,128)}, u32[]{:S(2)}) %copy-start.3) | copy-done | bytes 280
  18.6 0.0 copy-start.4
  18.6 0.7 %copy-done.4 = f32[128]{0:T(128)S(1)} copy-done((f32[128]{0:T(128)S(1)}, f32[128]{0:T(128)}, u32[]{:S(2)}) %copy-start.4) | copy-done | bytes 536
  19.3 0.5 prepare.1
  19.7 0.0 collective-permute-done.refs_1_
  19.7 0.0 collective-permute-done.2.refs_3_
  19.8 0.0 copy-start.1
  19.8 0.8 %copy-done.1 = f32[40,256]{1,0:T(8,128)S(1)} copy-done((f32[40,256]{1,0:T(8,128)S(1)}, f32[40,256]{1,0:T(8,128)}, u32[]{:S(2)}) %copy-start.1) | copy-done | bytes 40984
  20.5 0.6 basis.1
  21.1 3.7 %all-to-all-done = bf16[32,8,896]{2,1,0:T(8,128)(2,1)S(1)} async-done(((bf16[32,8,896]{2,1,0:T(8,128)(2,1)}), bf16[32,8,896]{2,1,0:T(8,128)(2,1)S(1)}, u32[]{:S(2)}, u32[]{:S(2)}) %all-to-all-start) | async-done | bytes 458784 | tf_op jit(solution)/shard_map/all_to_all | solution.py:360
  24.8 5.0 %forward.1 = (bf16[32,1024]{1,0:T(8,128)(2,1)S(1)}, bf16[8,256,1024]{2,1,0:T(8,128)(2,1)S(1)}, f32[8,160,1024]{2,1,0:T(8,128)S(1)}) custom-call(bf16[256,896]{1,0:T(8,128)(2,1)S(1)} %bitcast.8, f32[8,32,1024]{2,1,0:T(8,128)S(1)} %get-tuple-element.19.y_ref.refs_7_, s32[8,1024]{1,0:T(8,128)S(1)} %get-tuple-element.20.atoms_ref, ...), custom_call_target="tpu_custom_call" | custom-call | tf_op jit(solution)/shard_map/forward/pallas_call | solution.py:391
  29.8 0.8 %collective-permute-start.4 = (bf16[32,1024]{1,0:T(8,128)(2,1)S(1)}, bf16[32,1024]{1,0:T(8,128)(2,1)S(1)}, u32[]{:S(2)}, u32[]{:S(2)}) collective-permute-start(bf16[32,1024]{1,0:T(8,128)(2,1)S(1)} %get-tuple-element.23.refs_0_), channel_id=1, source_target_pairs={{0,2},{1,3},{2,0},{3,1},{4,6},{5,7},{6,4},{7,5},{8,10},{9,11},{10,... | collective-permute-start | bytes 196616 | tf_op jit(solution)/shard_map/ppermute | solution.py:306
  30.6 0.2 collective-permute-start.3
  30.8 3.4 %collective-permute-done.4.refs_2_ = bf16[32,1024]{1,0:T(8,128)(2,1)S(1)} collective-permute-done((bf16[32,1024]{1,0:T(8,128)(2,1)S(1)}, bf16[32,1024]{1,0:T(8,128)(2,1)S(1)}, u32[]{:S(2)}, u32[]{:S(2)}) %collective-permute-start.4) | collective-permute-done | bytes 65568 | tf_op jit(solution)/shard_map/ppermute | solution.py:306
  34.2 0.0 collective-permute-start.5
  34.2 0.0 collective-permute-done.3.refs_1_
  34.2 1.2 %collective-permute-done.5.refs_3_ = bf16[32,1024]{1,0:T(8,128)(2,1)S(1)} collective-permute-done((bf16[32,1024]{1,0:T(8,128)(2,1)S(1)}, bf16[32,1024]{1,0:T(8,128)(2,1)S(1)}, u32[]{:S(2)}, u32[]{:S(2)}) %collective-permute-start.5) | collective-permute-done | bytes 65568 | tf_op jit(solution)/shard_map/ppermute | solution.py:306
  35.4 4.7 %backward.1 = (bf16[256,896]{1,0:T(8,128)(2,1)S(1)}, f32[1,256]{1,0:T(1,128)}) custom-call(s32[1]{0:T(128)} %bitcast.me_ref, bf16[32,1024]{1,0:T(8,128)(2,1)S(1)} %get-tuple-element.23.refs_0_, bf16[32,1024]{1,0:T(8,128)(2,1)S(1)} %collective-permute-done.3.refs_1_, bf16[32,1024]{1,0:T(8,128)(2,1)S(1)} %collective-permute-done.4.refs_2_, ...), custom_call_target="tpu_custom_call" | custom-call | tf_op jit(solution)/shard_map/backward/pallas_call | solution.py:409
  40.1 17.0 %all_to_all.22 = bf16[32,8,896]{2,1,0:T(8,128)(2,1)S(1)} all-to-all(bf16[32,8,896]{2,1,0:T(8,128)(2,1)S(1)} %bitcast.10), channel_id=1, replica_groups=mesh['slab'=8,'dom'=4] {'slab','dom'}, dimensions={0} | all-to-all | bytes 917504 | tf_op jit(solution)/shard_map/all_to_all | solution.py:431
  57.1 1.5 %unpack.1 = f32[128,3200]{1,0:T(8,128)} custom-call(bf16[256,896]{1,0:T(8,128)(2,1)S(1)} %bitcast.9, bf16[128,64]{1,0:T(8,128)(2,1)S(1)} %get-tuple-element.31.turned_ref), custom_call_target="tpu_custom_call" | custom-call | tf_op jit(solution)/shard_map/unpack/pallas_call | solution.py:432
Async XLA Ops:
  3.2 21.7 %all-to-all-start = ((bf16[32,8,896]{2,1,0:T(8,128)(2,1)}), bf16[32,8,896]{2,1,0:T(8,128)(2,1)S(1)}, u32[]{:S(2)}, u32[]{:S(2)}) async-start(bf16[32,8,896]{2,1,0:T(8,128)(2,1)} %bitcast.12), calls=%async_computation | async-start | bytes 917504 | tf_op jit(solution)/shard_map/all_to_all | solution.py:360
  10.5 5.9 %collective-permute-start.1 = (f32[40,256]{1,0:T(8,128)}, f32[40,256]{1,0:T(8,128)S(1)}, u32[]{:S(2)}, u32[]{:S(2)}) collective-permute-start(f32[40,256]{1,0:T(8,128)} %get-tuple-element.18.refs_0_), channel_id=1, source_target_pairs={{0,2},{1,3},{2,0},{3,1},{4,6},{5,7},{6,4},{7,5},{8,10},{9,11},{10,... | collective-permute-start | bytes 122888 | tf_op jit(solution)/shard_map/ppermute | solution.py:306
  12.3 7.4 %collective-permute-start = (f32[40,256]{1,0:T(8,128)}, f32[40,256]{1,0:T(8,128)S(1)}, u32[]{:S(2)}, u32[]{:S(2)}) collective-permute-start(f32[40,256]{1,0:T(8,128)} %get-tuple-element.18.refs_0_), channel_id=1, source_target_pairs={{0,1},{1,0},{2,3},{3,2},{4,5},{5,4},{6,7},{7,6},{8,9},{9,8},{10,11... | collective-permute-start | bytes 122888 | tf_op jit(solution)/shard_map/ppermute | solution.py:306
  16.3 3.4 %collective-permute-start.2 = (f32[40,256]{1,0:T(8,128)S(1)}, f32[40,256]{1,0:T(8,128)S(1)}, u32[]{:S(2)}, u32[]{:S(2)}) collective-permute-start(f32[40,256]{1,0:T(8,128)S(1)} %collective-permute-done.1.refs_2_), channel_id=1, source_target_pairs={{0,1},{1,0},{2,3},{3,2},{4,5},{5,4},{6,7},{7,6},{8,9},{9,8},{10,11... | collective-permute-start | bytes 122888 | tf_op jit(solution)/shard_map/ppermute | solution.py:306
  16.4 0.8 %copy-start = (f32[128,128]{1,0:T(8,128)S(1)}, f32[128,128]{1,0:T(8,128)}, u32[]{:S(2)}) copy-start(f32[128,128]{1,0:T(8,128)} %pw_ref.1) | copy-start | bytes 196612
  17.2 0.7 %copy-start.2 = (f32[8,640]{1,0:T(8,128)S(1)}, f32[8,640]{1,0:T(8,128)}, u32[]{:S(2)}) copy-start(f32[8,640]{1,0:T(8,128)} %weight_ref.1) | copy-start | bytes 61444
  17.9 0.7 %copy-start.3 = (s32[8,1,8]{2,1,0:T(1,128)S(1)}, s32[8,1,8]{2,1,0:T(1,128)}, u32[]{:S(2)}) copy-start(s32[8,1,8]{2,1,0:T(1,128)} %halo_ref.1) | copy-start | bytes 772
  18.6 0.7 %copy-start.4 = (f32[128]{0:T(128)S(1)}, f32[128]{0:T(128)}, u32[]{:S(2)}) copy-start(f32[128]{0:T(128)} %param.14) | copy-start | bytes 1540
  19.8 0.8 %copy-start.1 = (f32[40,256]{1,0:T(8,128)S(1)}, f32[40,256]{1,0:T(8,128)}, u32[]{:S(2)}) copy-start(f32[40,256]{1,0:T(8,128)} %get-tuple-element.18.refs_0_) | copy-start | bytes 122884
  29.8 4.3 %collective-permute-start.4 = (bf16[32,1024]{1,0:T(8,128)(2,1)S(1)}, bf16[32,1024]{1,0:T(8,128)(2,1)S(1)}, u32[]{:S(2)}, u32[]{:S(2)}) collective-permute-start(bf16[32,1024]{1,0:T(8,128)(2,1)S(1)} %get-tuple-element.23.refs_0_), channel_id=1, source_target_pairs={{0,2},{1,3},{2,0},{3,1},{4,6},{5,7},{6,4},{7,5},{8,10},{9,11},{10,... | collective-permute-start | bytes 196616 | tf_op jit(solution)/shard_map/ppermute | solution.py:306
  30.6 3.6 %collective-permute-start.3 = (bf16[32,1024]{1,0:T(8,128)(2,1)S(1)}, bf16[32,1024]{1,0:T(8,128)(2,1)S(1)}, u32[]{:S(2)}, u32[]{:S(2)}) collective-permute-start(bf16[32,1024]{1,0:T(8,128)(2,1)S(1)} %get-tuple-element.23.refs_0_), channel_id=1, source_target_pairs={{0,1},{1,0},{2,3},{3,2},{4,5},{5,4},{6,7},{7,6},{8,9},{9,8},{10,11... | collective-permute-start | bytes 196616 | tf_op jit(solution)/shard_map/ppermute | solution.py:306
  34.2 1.3 %collective-permute-start.5 = (bf16[32,1024]{1,0:T(8,128)(2,1)S(1)}, bf16[32,1024]{1,0:T(8,128)(2,1)S(1)}, u32[]{:S(2)}, u32[]{:S(2)}) collective-permute-start(bf16[32,1024]{1,0:T(8,128)(2,1)S(1)} %collective-permute-done.4.refs_2_), channel_id=1, source_target_pairs={{0,1},{1,0},{2,3},{3,2},{4,5},{5,4},{6,7},{7,6},{8,9},{9,8},{10,11... | collective-permute-start | bytes 196616 | tf_op jit(solution)/shard_map/ppermute | solution.py:306

commit v6 on v5

--- a/solution.py
+++ b/solution.py
@@ -238,7 +238,7 @@
     for k in range(slots):
         hot = onehot_of(k, atoms_ref, table, slice(None))
         rad = radial(k, slots, w_ref, b_ref, slice(None))
-        hot_ref[k] = hot
+        hot_ref[:, k * hot.shape[1] : (k + 1) * hot.shape[1]] = hot
         r_ref[k] = rad
         got = dot_tn(h_ref[:, 0 : COMPONENTS * quarter], hot)
         acc = total[...]
@@ -260,7 +260,7 @@
     sums = refs[:parts]
     pw_ref, own_ref, cot_ref, y_ref, hot_ref, r_ref = refs[parts : parts + 6]
     grads_ref, density_ref, s_all, ds, z, acc, dens = refs[parts + 6 :]
-    slots = y_ref.shape[0]
+    slots, width = y_ref.shape[0], y_ref.shape[2]
     me = me_ref[0]
     channels = parts * quarter
     for j in range(parts):
@@ -284,10 +284,11 @@
             first, last = degree * degree, (degree + 1) ** 2
             weighted = ds[...] * r_ref[k, degree * quarter : (degree + 1) * quarter, :]
             for m in range(first, last):
-                z[m * quarter : (m + 1) * quarter, :] = (
+                z[m * quarter : (m + 1) * quarter, k % 2 * width : (k % 2 + 1) * width] = (
                     weighted * y_ref[k, m : m + 1, :]
                 ).astype(BF)
-        acc[...] += dot_nt(z[...], hot_ref[k])
+        if k % 2 == 1:
+            acc[...] += dot_nt(z[...], hot_ref[:, (k - 1) * width : (k + 1) * width])
 
     filled = (COMPONENTS * quarter) // 128 * 128
     grads_ref[:, 0:filled] = acc[0:filled, :].T.astype(BF)
@@ -332,7 +333,7 @@
     me = lax.axis_index("dom").astype(jnp.int32).reshape(1)
     groups = -(-COMPONENTS // n_dom)
     wide = pltpu.CompilerParams(vmem_limit_bytes=56 * 2**20)
-    narrow = pltpu.CompilerParams(vmem_limit_bytes=(16 if table <= 256 else 56) * 2**20)
+    narrow = pltpu.CompilerParams(vmem_limit_bytes=(28 if table <= 256 else 56) * 2**20)
     vmem = pl.BlockSpec(memory_space=pltpu.VMEM)
     smem = pl.BlockSpec(memory_space=pltpu.SMEM)
     any_space = pl.BlockSpec(memory_space=pl.ANY)
@@ -394,7 +395,7 @@
         out_specs=[vmem] * 3,
         out_shape=[
             jax.ShapeDtypeStruct((quarter, slab_probes), BF),
-            jax.ShapeDtypeStruct((slots, table, slab_probes), BF),
+            jax.ShapeDtypeStruct((table, slots * slab_probes), BF),
             jax.ShapeDtypeStruct((slots, 5 * quarter, slab_probes), F32),
         ],
         scratch_shapes=[
@@ -413,7 +414,7 @@
         scratch_shapes=[
             pltpu.VMEM((channels, slab_probes), F32),
             pltpu.VMEM((quarter, slab_probes), F32),
-            pltpu.VMEM((COMPONENTS * quarter, slab_probes), BF),
+            pltpu.VMEM((COMPONENTS * quarter, 2 * slab_probes), BF),
             pltpu.VMEM((COMPONENTS * quarter, table), F32),
             pltpu.VMEM((1, slab_probes), F32),
         ],

time: 59.1 us -> 59.1 us (level)
  no operation moved by 1% of the time
where the time goes in v6:
time: 59.1 us; the launch traced here: 58.6 us
  blocking collectives  17 us (29%)
  Pallas kernels  14.7 us (25%)
  waiting for transfers between devices  12.4 us (21%)
  starting transfers between devices  10.1 us (17%)
  local copies, waits for them, and re-layouts  3.68 us (6%)
  between operations  0.71 us (1%)
    all_to_all x1, blocking collectives, shards(): lax.all_to_all(grads, ('slab', 'dom'), split_axis=0, concat_axis=0, tiled...  17 us
    ppermute x6, waiting for transfers between devices, spread_over(): blocks[j | bit] = lax.ppermute(blocks[j], 'dom', pairs)  8.69 us
    all_to_all x1, starting transfers between devices, shards(): lax.all_to_all(send, ('slab', 'dom'), split_axis=0, concat_axis=0, tiled=...  7.3 us
    pallas_call x1, Pallas kernels, shards(): pl.pallas_call(functools.partial(forward_kernel, quarter), in_specs=[vmem...  4.99 us
    pallas_call x1, Pallas kernels, shards(): pl.pallas_call(functools.partial(backward_kernel, n_dom, quarter, probes)...  4.68 us
    all_to_all x1, waiting for transfers between devices, shards(): lax.all_to_all(send, ('slab', 'dom'), split_axis=0, concat_axis=0, tiled=...  3.73 us
    unnamed x10, local copies, waits for them, and re-layouts  3.68 us
    ppermute x6, starting transfers between devices, spread_over(): blocks[j | bit] = lax.ppermute(blocks[j], 'dom', pairs)  2.77 us
  transfers between devices with their start and end apart: 7, of which 4 were waited for; matrix products, arithmetic and copies ran while one was open for 0% of the time, Pallas kernels for 2%

profile of v6, /device:TPU:0, one launch (start us, length us, event | category | flops | bytes accessed | tf_op | source)
XLA Modules:
  0.0 58.6 jit_solution(13991452813980832979)
XLA Ops:
  0.6 2.5 %pack.1 = (bf16[256,896]{1,0:T(8,128)(2,1)}, f32[40,256]{1,0:T(8,128)}) custom-call(bf16[128,3200]{1,0:T(8,128)(2,1)} %h_hbm.1, s32[8,1,8]{2,1,0:T(1,128)} %halo_ref.1, f32[3,8,256]{2,1,0:T(8,128)} %off_hbm.1, s32[8,256]{1,0:T(8,128)} %atoms_hbm.1, f32[1,256]{1,0:T(1,128)} %bitcast.13), custom_call_target="tpu_custom_call" | custom-call | tf_op jit(solution)/shard_map/pack/pallas_call | solution.py:341
  3.2 7.3 %all-to-all-start = ((bf16[32,8,896]{2,1,0:T(8,128)(2,1)}), bf16[32,8,896]{2,1,0:T(8,128)(2,1)S(1)}, u32[]{:S(2)}, u32[]{:S(2)}) async-start(bf16[32,8,896]{2,1,0:T(8,128)(2,1)} %bitcast.12), calls=%async_computation | async-start | bytes 917504 | tf_op jit(solution)/shard_map/all_to_all | solution.py:361
  10.5 1.8 %collective-permute-start.1 = (f32[40,256]{1,0:T(8,128)}, f32[40,256]{1,0:T(8,128)S(1)}, u32[]{:S(2)}, u32[]{:S(2)}) collective-permute-start(f32[40,256]{1,0:T(8,128)} %get-tuple-element.18.refs_0_), channel_id=1, source_target_pairs={{0,2},{1,3},{2,0},{3,1},{4,6},{5,7},{6,4},{7,5},{8,10},{9,11},{10,... | collective-permute-start | bytes 122888 | tf_op jit(solution)/shard_map/ppermute | solution.py:307
  12.3 0.0 collective-permute-start
  12.3 4.0 %collective-permute-done.1.refs_2_ = f32[40,256]{1,0:T(8,128)S(1)} collective-permute-done((f32[40,256]{1,0:T(8,128)}, f32[40,256]{1,0:T(8,128)S(1)}, u32[]{:S(2)}, u32[]{:S(2)}) %collective-permute-start.1) | collective-permute-done | bytes 40992 | tf_op jit(solution)/shard_map/ppermute | solution.py:307
  16.3 0.0 collective-permute-start.2
  16.4 0.0 copy-start
  16.4 0.8 %copy-done = f32[128,128]{1,0:T(8,128)S(1)} copy-done((f32[128,128]{1,0:T(8,128)S(1)}, f32[128,128]{1,0:T(8,128)}, u32[]{:S(2)}) %copy-start) | copy-done | bytes 65560
  17.2 0.0 copy-start.2
  17.2 0.7 %copy-done.2 = f32[8,640]{1,0:T(8,128)S(1)} copy-done((f32[8,640]{1,0:T(8,128)S(1)}, f32[8,640]{1,0:T(8,128)}, u32[]{:S(2)}) %copy-start.2) | copy-done | bytes 20504
  17.9 0.0 copy-start.3
  17.9 0.7 %copy-done.3 = s32[8,1,8]{2,1,0:T(1,128)S(1)} copy-done((s32[8,1,8]{2,1,0:T(1,128)S(1)}, s32[8,1,8]{2,1,0:T(1,128)}, u32[]{:S(2)}) %copy-start.3) | copy-done | bytes 280
  18.6 0.0 copy-start.4
  18.6 0.7 %copy-done.4 = f32[128]{0:T(128)S(1)} copy-done((f32[128]{0:T(128)S(1)}, f32[128]{0:T(128)}, u32[]{:S(2)}) %copy-start.4) | copy-done | bytes 536
  19.3 0.5 prepare.1
  19.7 0.0 collective-permute-done.refs_1_
  19.7 0.0 collective-permute-done.2.refs_3_
  19.8 0.0 copy-start.1
  19.8 0.8 %copy-done.1 = f32[40,256]{1,0:T(8,128)S(1)} copy-done((f32[40,256]{1,0:T(8,128)S(1)}, f32[40,256]{1,0:T(8,128)}, u32[]{:S(2)}) %copy-start.1) | copy-done | bytes 40984
  20.5 0.6 basis.1
  21.1 3.7 %all-to-all-done = bf16[32,8,896]{2,1,0:T(8,128)(2,1)S(1)} async-done(((bf16[32,8,896]{2,1,0:T(8,128)(2,1)}), bf16[32,8,896]{2,1,0:T(8,128)(2,1)S(1)}, u32[]{:S(2)}, u32[]{:S(2)}) %all-to-all-start) | async-done | bytes 458784 | tf_op jit(solution)/shard_map/all_to_all | solution.py:361
  24.8 5.0 %forward.1 = (bf16[32,1024]{1,0:T(8,128)(2,1)S(1)}, bf16[256,8192]{1,0:T(8,128)(2,1)S(1)}, f32[8,160,1024]{2,1,0:T(8,128)S(1)}) custom-call(bf16[256,896]{1,0:T(8,128)(2,1)S(1)} %bitcast.8, f32[8,32,1024]{2,1,0:T(8,128)S(1)} %get-tuple-element.19.y_ref.refs_7_, s32[8,1024]{1,0:T(8,128)S(1)} %get-tuple-element.20.atoms_ref, ...), custom_call_target="tpu_custom_call" | custom-call | tf_op jit(solution)/shard_map/forward/pallas_call | solution.py:392
  29.8 0.8 %collective-permute-start.4 = (bf16[32,1024]{1,0:T(8,128)(2,1)S(1)}, bf16[32,1024]{1,0:T(8,128)(2,1)S(1)}, u32[]{:S(2)}, u32[]{:S(2)}) collective-permute-start(bf16[32,1024]{1,0:T(8,128)(2,1)S(1)} %get-tuple-element.23.refs_0_), channel_id=1, source_target_pairs={{0,2},{1,3},{2,0},{3,1},{4,6},{5,7},{6,4},{7,5},{8,10},{9,11},{10,... | collective-permute-start | bytes 196616 | tf_op jit(solution)/shard_map/ppermute | solution.py:307
  30.6 0.2 collective-permute-start.3
  30.8 3.4 %collective-permute-done.4.refs_2_ = bf16[32,1024]{1,0:T(8,128)(2,1)S(1)} collective-permute-done((bf16[32,1024]{1,0:T(8,128)(2,1)S(1)}, bf16[32,1024]{1,0:T(8,128)(2,1)S(1)}, u32[]{:S(2)}, u32[]{:S(2)}) %collective-permute-start.4) | collective-permute-done | bytes 65568 | tf_op jit(solution)/shard_map/ppermute | solution.py:307
  34.2 0.0 collective-permute-start.5
  34.2 0.0 collective-permute-done.3.refs_1_
  34.2 1.2 %collective-permute-done.5.refs_3_ = bf16[32,1024]{1,0:T(8,128)(2,1)S(1)} collective-permute-done((bf16[32,1024]{1,0:T(8,128)(2,1)S(1)}, bf16[32,1024]{1,0:T(8,128)(2,1)S(1)}, u32[]{:S(2)}, u32[]{:S(2)}) %collective-permute-start.5) | collective-permute-done | bytes 65568 | tf_op jit(solution)/shard_map/ppermute | solution.py:307
  35.4 4.7 %backward.1 = (bf16[256,896]{1,0:T(8,128)(2,1)S(1)}, f32[1,256]{1,0:T(1,128)}) custom-call(s32[1]{0:T(128)} %bitcast.me_ref, bf16[32,1024]{1,0:T(8,128)(2,1)S(1)} %get-tuple-element.23.refs_0_, bf16[32,1024]{1,0:T(8,128)(2,1)S(1)} %collective-permute-done.3.refs_1_, bf16[32,1024]{1,0:T(8,128)(2,1)S(1)} %collective-permute-done.4.refs_2_, ...), custom_call_target="tpu_custom_call" | custom-call | tf_op jit(solution)/shard_map/backward/pallas_call | solution.py:410
  40.1 17.0 %all_to_all.22 = bf16[32,8,896]{2,1,0:T(8,128)(2,1)S(1)} all-to-all(bf16[32,8,896]{2,1,0:T(8,128)(2,1)S(1)} %bitcast.10), channel_id=1, replica_groups=mesh['slab'=8,'dom'=4] {'slab','dom'}, dimensions={0} | all-to-all | bytes 917504 | tf_op jit(solution)/shard_map/all_to_all | solution.py:432
  57.1 1.5 %unpack.1 = f32[128,3200]{1,0:T(8,128)} custom-call(bf16[256,896]{1,0:T(8,128)(2,1)S(1)} %bitcast.9, bf16[128,64]{1,0:T(8,128)(2,1)S(1)} %get-tuple-element.31.turned_ref), custom_call_target="tpu_custom_call" | custom-call | tf_op jit(solution)/shard_map/unpack/pallas_call | solution.py:433
Async XLA Ops:
  3.2 21.7 %all-to-all-start = ((bf16[32,8,896]{2,1,0:T(8,128)(2,1)}), bf16[32,8,896]{2,1,0:T(8,128)(2,1)S(1)}, u32[]{:S(2)}, u32[]{:S(2)}) async-start(bf16[32,8,896]{2,1,0:T(8,128)(2,1)} %bitcast.12), calls=%async_computation | async-start | bytes 917504 | tf_op jit(solution)/shard_map/all_to_all | solution.py:361
  10.5 5.9 %collective-permute-start.1 = (f32[40,256]{1,0:T(8,128)}, f32[40,256]{1,0:T(8,128)S(1)}, u32[]{:S(2)}, u32[]{:S(2)}) collective-permute-start(f32[40,256]{1,0:T(8,128)} %get-tuple-element.18.refs_0_), channel_id=1, source_target_pairs={{0,2},{1,3},{2,0},{3,1},{4,6},{5,7},{6,4},{7,5},{8,10},{9,11},{10,... | collective-permute-start | bytes 122888 | tf_op jit(solution)/shard_map/ppermute | solution.py:307
  12.3 7.4 %collective-permute-start = (f32[40,256]{1,0:T(8,128)}, f32[40,256]{1,0:T(8,128)S(1)}, u32[]{:S(2)}, u32[]{:S(2)}) collective-permute-start(f32[40,256]{1,0:T(8,128)} %get-tuple-element.18.refs_0_), channel_id=1, source_target_pairs={{0,1},{1,0},{2,3},{3,2},{4,5},{5,4},{6,7},{7,6},{8,9},{9,8},{10,11... | collective-permute-start | bytes 122888 | tf_op jit(solution)/shard_map/ppermute | solution.py:307
  16.3 3.4 %collective-permute-start.2 = (f32[40,256]{1,0:T(8,128)S(1)}, f32[40,256]{1,0:T(8,128)S(1)}, u32[]{:S(2)}, u32[]{:S(2)}) collective-permute-start(f32[40,256]{1,0:T(8,128)S(1)} %collective-permute-done.1.refs_2_), channel_id=1, source_target_pairs={{0,1},{1,0},{2,3},{3,2},{4,5},{5,4},{6,7},{7,6},{8,9},{9,8},{10,11... | collective-permute-start | bytes 122888 | tf_op jit(solution)/shard_map/ppermute | solution.py:307
  16.4 0.8 %copy-start = (f32[128,128]{1,0:T(8,128)S(1)}, f32[128,128]{1,0:T(8,128)}, u32[]{:S(2)}) copy-start(f32[128,128]{1,0:T(8,128)} %pw_ref.1) | copy-start | bytes 196612
  17.2 0.7 %copy-start.2 = (f32[8,640]{1,0:T(8,128)S(1)}, f32[8,640]{1,0:T(8,128)}, u32[]{:S(2)}) copy-start(f32[8,640]{1,0:T(8,128)} %weight_ref.1) | copy-start | bytes 61444
  17.9 0.7 %copy-start.3 = (s32[8,1,8]{2,1,0:T(1,128)S(1)}, s32[8,1,8]{2,1,0:T(1,128)}, u32[]{:S(2)}) copy-start(s32[8,1,8]{2,1,0:T(1,128)} %halo_ref.1) | copy-start | bytes 772
  18.6 0.7 %copy-start.4 = (f32[128]{0:T(128)S(1)}, f32[128]{0:T(128)}, u32[]{:S(2)}) copy-start(f32[128]{0:T(128)} %param.14) | copy-start | bytes 1540
  19.8 0.8 %copy-start.1 = (f32[40,256]{1,0:T(8,128)S(1)}, f32[40,256]{1,0:T(8,128)}, u32[]{:S(2)}) copy-start(f32[40,256]{1,0:T(8,128)} %get-tuple-element.18.refs_0_) | copy-start | bytes 122884
  29.8 4.3 %collective-permute-start.4 = (bf16[32,1024]{1,0:T(8,128)(2,1)S(1)}, bf16[32,1024]{1,0:T(8,128)(2,1)S(1)}, u32[]{:S(2)}, u32[]{:S(2)}) collective-permute-start(bf16[32,1024]{1,0:T(8,128)(2,1)S(1)} %get-tuple-element.23.refs_0_), channel_id=1, source_target_pairs={{0,2},{1,3},{2,0},{3,1},{4,6},{5,7},{6,4},{7,5},{8,10},{9,11},{10,... | collective-permute-start | bytes 196616 | tf_op jit(solution)/shard_map/ppermute | solution.py:307
  30.6 3.6 %collective-permute-start.3 = (bf16[32,1024]{1,0:T(8,128)(2,1)S(1)}, bf16[32,1024]{1,0:T(8,128)(2,1)S(1)}, u32[]{:S(2)}, u32[]{:S(2)}) collective-permute-start(bf16[32,1024]{1,0:T(8,128)(2,1)S(1)} %get-tuple-element.23.refs_0_), channel_id=1, source_target_pairs={{0,1},{1,0},{2,3},{3,2},{4,5},{5,4},{6,7},{7,6},{8,9},{9,8},{10,11... | collective-permute-start | bytes 196616 | tf_op jit(solution)/shard_map/ppermute | solution.py:307
  34.2 1.3 %collective-permute-start.5 = (bf16[32,1024]{1,0:T(8,128)(2,1)S(1)}, bf16[32,1024]{1,0:T(8,128)(2,1)S(1)}, u32[]{:S(2)}, u32[]{:S(2)}) collective-permute-start(bf16[32,1024]{1,0:T(8,128)(2,1)S(1)} %collective-permute-done.4.refs_2_), channel_id=1, source_target_pairs={{0,1},{1,0},{2,3},{3,2},{4,5},{5,4},{6,7},{7,6},{8,9},{9,8},{10,11... | collective-permute-start | bytes 196616 | tf_op jit(solution)/shard_map/ppermute | solution.py:307
